TPU v7x, 256 devices: a whole 4x4x8 slice. The times are simulated.
256 devices in a mesh: lat: 32 (over z, x), lon: 2 (over core), frame: 4 (over y).
Axes of the slice: x: 4, y: 4, z: 8, core: 2. Of those that a mesh axis runs over, the one named last changes fastest.
Arguments:
- frames_in: bfloat16 [4, 512, 32, 1024], P('frame', 'lat', 'lon'), may hold values from -64 to 64
- w_query: bfloat16 [1024, 1024], replicated
- w_key: bfloat16 [1024, 1024], replicated
- w_value: bfloat16 [1024, 1024], replicated, may hold values from -0.1875 to 0.1875
- w_out: bfloat16 [1024, 1024], replicated, may hold values from -0.1875 to 0.1875
- codes: int32 [4, 64, 4, 9], P('frame', 'lat', 'lon'), may hold values from 0 to 8, as said below
- counts: int32 [4, 64, 4], P('frame', 'lat', 'lon'), may hold values from 3 to 9, as said below
Outputs:
- output: bfloat16 [4, 512, 32, 1024], P('frame', 'lat', 'lon')
Inputs may be any that keep to these rules, and one draw needn't show every extreme that they name: codes[f, r, c] holds each of the nine window positions 0 to 8 once; position code means window row code // 3 and window column code % 3. counts is 6 to 9 in the first and the last 16 tile rows and 3 to 6 in the others.
All inputs are finite; a program needn't handle non-finite values.
Results may differ from a plain program's by a relative error of at most 0.008.
Values may be sent and summed in bfloat16 or wider, within the bound.
A program may use at most 192 MiB of HBM per device.

v0:
```python
import math

import jax
import jax.numpy as jnp
from jax import lax
from jax.sharding import PartitionSpec as P

HEADS = 16
HEAD = 64
TILE = 8
WIN = 9


def extended(block, sides, width, periodic):
    for axis, dim in sides:
        count = lax.axis_size(axis)
        forward = [(i, i + 1) for i in range(count - 1)]
        if periodic:
            forward.append((count - 1, 0))
        backward = [(target, source) for source, target in forward]
        low = lax.ppermute(
            lax.slice_in_dim(block, block.shape[dim] - width, None, axis=dim), axis, forward
        )
        high = lax.ppermute(lax.slice_in_dim(block, 0, width, axis=dim), axis, backward)
        block = jnp.concatenate([low, block, high], axis=dim)
    return block


def passed_along(value, axis, steps):
    count = lax.axis_size(axis)
    initial, last = (max(0, -steps), min(count, count - steps))
    return lax.ppermute(value, axis, [(source, source + steps) for source in range(initial, last)])


def project_pair(inputs, w_key, w_value):
    key_part = jnp.dot(inputs, w_key, preferred_element_type=jnp.float32).astype(jnp.bfloat16)
    value_part = jnp.dot(inputs, w_value, preferred_element_type=jnp.float32).astype(jnp.bfloat16)
    return jnp.concatenate([key_part, value_part], axis=-1)


def rims(rim_input):
    widened = extended(rim_input, (("lon", 2),), TILE, True)
    return extended(widened, (("lat", 1),), TILE, False)


def on_device(frames_in, w_query, w_key, w_value, w_out, codes, counts):
    grid_cells = frames_in[0]
    lat_cells, lon_cells, feature_dim = grid_cells.shape
    rows_tile = lat_cells // TILE
    cols_tile = lon_cells // TILE
    tile_count = rows_tile * cols_tile
    queries_all = jnp.dot(grid_cells, w_query, preferred_element_type=jnp.float32).astype(
        jnp.bfloat16
    )
    own_pairs = project_pair(grid_cells, w_key, w_value)
    earlier_pairs = passed_along(own_pairs, "frame", 1)
    rimmed = rims(jnp.stack([own_pairs, earlier_pairs]))
    rim_rows = rows_tile + 2
    rim_cols = cols_tile + 2
    tiled_pairs = rimmed.reshape(2, rim_rows, TILE, rim_cols, TILE, 2 * feature_dim)
    tiled_pairs = tiled_pairs.transpose(0, 1, 3, 2, 4, 5).reshape(
        2, rim_rows * rim_cols, TILE * TILE, 2 * feature_dim
    )
    queries = queries_all.reshape(rows_tile, TILE, cols_tile, TILE, HEADS, HEAD)
    queries = queries.transpose(0, 2, 1, 3, 4, 5).reshape(tile_count, TILE * TILE, HEADS, HEAD)
    lat_index = lax.axis_index("lat")
    tile_rows_all = rows_tile * lax.axis_size("lat")
    global_rows = lat_index * rows_tile + jnp.arange(rows_tile, dtype=jnp.int32)
    first_rows = jnp.clip(global_rows - 1, 0, tile_rows_all - 3) - lat_index * rows_tile + 1
    slot_codes = codes[0]
    tile_rows = first_rows[:, None, None] + slot_codes // 3
    tile_cols = jnp.arange(cols_tile, dtype=jnp.int32)[None, :, None] + slot_codes % 3
    slot_tiles = (tile_rows * rim_cols + tile_cols).reshape(tile_count, WIN)
    live_slots = jnp.arange(WIN, dtype=jnp.int32)[None, :] < counts[0].reshape(tile_count)[:, None]
    earlier_ok = lax.axis_index("frame") > 0
    live_both = jnp.stack([live_slots, jnp.logical_and(live_slots, earlier_ok)], axis=1)
    group_size = math.gcd(tile_count, 4)
    block_count = tile_count // group_size
    score_scale = 1.0 / math.sqrt(HEAD)

    def attend(operands):
        block_q, block_tiles, block_live = operands
        chosen = jnp.take(tiled_pairs, block_tiles.reshape(-1), axis=1)
        chosen = chosen.reshape(2, group_size, WIN, TILE * TILE, 2 * feature_dim)
        key_part = chosen[..., :feature_dim].reshape(2, group_size, WIN, TILE * TILE, HEADS, HEAD)
        value_part = chosen[..., feature_dim:].reshape(2, group_size, WIN, TILE * TILE, HEADS, HEAD)
        scores = (
            jnp.einsum("gqhd,sgjkhd->ghqsjk", block_q, key_part, preferred_element_type=jnp.float32)
            * score_scale
        )
        allowed = block_live[:, None, None, :, :, None]
        scores = jnp.where(allowed, scores, -1e30)
        row_max = jnp.max(scores, axis=(3, 4, 5), keepdims=True)
        exponent = jnp.exp(scores - row_max)
        denominator = jnp.sum(exponent, axis=(3, 4, 5))
        weights = exponent.astype(jnp.bfloat16)
        combined = jnp.einsum(
            "ghqsjk,sgjkhd->gqhd", weights, value_part, preferred_element_type=jnp.float32
        )
        combined = combined / jnp.transpose(denominator, (0, 2, 1))[..., None]
        return combined.astype(jnp.bfloat16).reshape(group_size, TILE * TILE, feature_dim)

    attended = lax.map(
        attend,
        (
            queries.reshape(block_count, group_size, TILE * TILE, HEADS, HEAD),
            slot_tiles.reshape(block_count, group_size, WIN),
            live_both.reshape(block_count, group_size, 2, WIN),
        ),
    )
    attended = attended.reshape(rows_tile, cols_tile, TILE, TILE, feature_dim)
    attended = attended.transpose(0, 2, 1, 3, 4).reshape(lat_cells, lon_cells, feature_dim)
    output = jnp.dot(attended, w_out, preferred_element_type=jnp.float32).astype(jnp.bfloat16)
    return output[None]


def solution(mesh):
    placed = (
        P("frame", "lat", "lon", None),
        P(),
        P(),
        P(),
        P(),
        P("frame", "lat", "lon", None),
        P("frame", "lat", "lon"),
    )
    return jax.shard_map(
        on_device,
        mesh=mesh,
        in_specs=placed,
        out_specs=P("frame", "lat", "lon", None),
        check_vma=False,
    )
```

profile of v0, /device:TPU:111, one launch (start us, length us, event | category | flops | bytes accessed | tf_op | source)
XLA Modules:
  0.0 262.8 jit_solution(12085458586592698808)
XLA Ops:
  0.0 0.0 copy-start
  0.0 1.6 copy-done
  1.6 1.7 fusion.21
  3.3 2.5 fusion.24
  5.8 0.1 fusion.47
  6.0 3.2 %collective-permute-start = (bf16[16,16,2048]{2,1,0:T(8,128)(2,1)S(1)}, bf16[16,16,2048]{2,1,0:T(8,128)(2,1)S(1)}, u32[]{:S(2)}, u32[]{:S(2)}) collective-permute-start(bf16[16,16,2048]{2,1,0:T(8,128)(2,1)S(1)} %get-tuple-element.32), channel_id=1, source_target_pairs={{0,1},{1,2},{2,3},{4,5},{5,6},{6,7},{8,9},{9,10},{10,11},{12,13},{... | collective-permute-start | bytes 3145736 | tf_op jit(solution)/shard_map/ppermute | solution.py:32
  9.2 22.7 %collective-permute-done = bf16[16,16,2048]{2,1,0:T(8,128)(2,1)S(1)} collective-permute-done((bf16[16,16,2048]{2,1,0:T(8,128)(2,1)S(1)}, bf16[16,16,2048]{2,1,0:T(8,128)(2,1)S(1)}, u32[]{:S(2)}, u32[]{:S(2)}) %collective-permute-start) | collective-permute-done | bytes 1048608 | tf_op jit(solution)/shard_map/ppermute | solution.py:32
  31.9 0.1 fusion.36
  32.1 1.6 collective-permute-start.1
  33.7 0.0 copy-start.5
  33.7 0.0 copy-start.7
  33.7 0.0 copy-start.6
  33.7 0.1 collective-permute-start.2
  33.8 2.2 collective-permute-done.1
  36.0 0.0 copy-start.2
  36.0 1.5 collective-permute-done.2
  37.5 0.0 copy-done.2
  37.5 0.0 copy-start.3
  37.5 1.0 copy-done.3
  38.5 0.4 pad_maximum_fusion.1
  39.0 2.5 fusion.49
  41.5 4.7 %collective-permute-start.3 = (bf16[2,8,32,2048]{3,2,1,0:T(8,128)(2,1)}, bf16[2,8,32,2048]{3,2,1,0:T(8,128)(2,1)}, u32[]{:S(2)}, u32[]{:S(2)}) collective-permute-start(bf16[2,8,32,2048]{3,2,1,0:T(8,128)(2,1)} %get-tuple-element.26), channel_id=1, source_target_pairs={{0,8},{8,16},{16,24},{24,32},{32,40},{40,48},{48,56},{56,64},{64,7... | collective-permute-start | bytes 6291464 | tf_op jit(solution)/shard_map/ppermute | solution.py:21
  46.1 2.1 collective-permute-start.4
  48.2 0.0 copy-done.5
  48.3 0.1 ne.74
  48.4 0.1 add.165
  48.4 0.1 add.166
  48.5 0.1 div.37
  48.6 0.1 rem.41
  48.7 0.1 add.169
  48.8 0.1 add.154
  48.9 0.1 add.155
  48.9 0.0 copy-done.7
  49.0 0.1 lt.60
  49.0 0.0 copy-done.6
  49.0 3.1 %fusion.27 = bf16[16,16,1024]{2,1,0:T(8,128)(2,1)} fusion(bf16[1024,1024]{1,0:T(8,128)(2,1)} %param.8, bf16[1,16,16,1024]{3,2,1,0:T(8,128)(2,1)S(1)} %copy-done.6), kind=kOutput, calls=%fused_computation.28 | convolution fusion | flops 537133056 | bytes 3145728 | tf_op jit(solution)/shard_map/dot_general | solution.py:52
  52.2 1.8 reshape.247
  53.9 1.3 copy.20
  55.2 0.1 iota_compare_fusion
  55.3 0.1 compare_and_fusion
  55.4 35.7 %collective-permute-done.3 = bf16[2,8,32,2048]{3,2,1,0:T(8,128)(2,1)} collective-permute-done((bf16[2,8,32,2048]{3,2,1,0:T(8,128)(2,1)}, bf16[2,8,32,2048]{3,2,1,0:T(8,128)(2,1)}, u32[]{:S(2)}, u32[]{:S(2)}) %collective-permute-start.3) | collective-permute-done | bytes 2097184 | tf_op jit(solution)/shard_map/ppermute | solution.py:21
  91.1 7.1 %collective-permute-done.4 = bf16[2,8,32,2048]{3,2,1,0:T(8,128)(2,1)} collective-permute-done((bf16[2,8,32,2048]{3,2,1,0:T(8,128)(2,1)}, bf16[2,8,32,2048]{3,2,1,0:T(8,128)(2,1)}, u32[]{:S(2)}, u32[]{:S(2)}) %collective-permute-start.4) | collective-permute-done | bytes 2097184 | tf_op jit(solution)/shard_map/ppermute | solution.py:24
  98.2 6.7 %pad_maximum_fusion = bf16[2,32,32,2048]{3,2,1,0:T(8,128)(2,1)} fusion(bf16[2,8,32,2048]{3,2,1,0:T(8,128)(2,1)} %collective-permute-done.4, bf16[2,16,8,2048]{3,2,1,0:T(8,128)(2,1)} %copy-done.3, bf16[1,16,16,2048]{3,2,1,0:T(8,128)(2,1)S(1)} %bitcast.76, bf16[1,16,16,2048]{3,2,1,0:T(8,128)(2,1)S(1)} %get-tuple-element.31, ...), kind=kLoop, calls=%fused_computation.12 | loop fusion | flops 50331648 | bytes 16777216 | tf_op jit(solution)/shard_map/concatenate | solution.py:25
  104.8 8.4 %copy.18 = bf16[2,4,8,4,8,2048]{5,4,2,3,1,0:T(8,128)(2,1)} copy(bf16[2,4,8,4,8,2048]{5,4,3,2,1,0:T(8,128)(2,1)} %bitcast.73) | data formatting | bytes 16777216 | tf_op jit(solution)/shard_map/reshape | solution.py:60
  113.2 11.4 %gather_fusion = bf16[36,2,64,2048]{3,2,1,0:T(8,128)(2,1)} fusion(bf16[2,16,64,2048]{3,2,1,0:T(8,128)(2,1)} %bitcast.71, s32[1024]{0:T(1024)S(1)} %pad_clamp_fusion), kind=kCustom, calls=%fused_computation | custom fusion | bytes 37748880 | tf_op jit(solution)/shard_map/while/body/eval_jaxpr/jit(_take)/gather | solution.py:83
  124.7 9.8 %copy_select_fusion = bf16[2,4,9,64,2048]{4,3,2,1,0:T(8,128)(2,1)S(1)} fusion(bf16[2,4,9,64,2048]{4,3,0,2,1:T(8,128)(2,1)} %bitcast.72, pred[4,9]{1,0:T(4,128)(4,1)S(1)} %compare_and_fusion), kind=kLoop, calls=%fused_computation.11 | loop fusion | flops 9437184 | bytes 37748772 | tf_op jit(solution)/shard_map/while/body/eval_jaxpr/jit(_take)/select_n | solution.py:83
  134.4 6.9 %fusion.48 = (bf16[2,4,9,64,1024]{4,3,2,1,0:T(8,128)(2,1)}, bf16[2,4,9,64,1024]{4,3,2,1,0:T(8,128)(2,1)}) fusion(bf16[2,4,9,64,2048]{4,3,2,1,0:T(8,128)(2,1)S(1)} %copy_select_fusion), kind=kLoop, calls=%fused_computation.60 | loop fusion | bytes 37748736 | tf_op jit(solution)/shard_map/while/body/eval_jaxpr/slice | solution.py:86
  141.3 24.7 %reshape.248 = bf16[2,4,9,64,16,64]{5,4,3,2,1,0:T(8,128)(2,1)} reshape(bf16[2,4,9,64,1024]{4,3,2,1,0:T(8,128)(2,1)} %get-tuple-element.24) | data formatting | bytes 18874368 | tf_op jit(solution)/shard_map/while/body/eval_jaxpr/reshape | solution.py:85
  166.0 0.0 copy-start.4
  166.0 24.7 %reshape.246 = bf16[2,4,9,64,16,64]{5,4,3,2,1,0:T(8,128)(2,1)} reshape(bf16[2,4,9,64,1024]{4,3,2,1,0:T(8,128)(2,1)} %get-tuple-element.17) | data formatting | bytes 18874368 | tf_op jit(solution)/shard_map/while/body/eval_jaxpr/reshape | solution.py:86
  190.8 0.0 copy-done.4
  190.8 21.2 %fusion = (f32[4,16,64]{2,1,0:T(8,128)S(1)}, f32[4,16,64,2,9,64]{2,5,4,3,1,0:T(8,128)}) fusion(pred[4,2,9]{2,1,0:T(4,128)(4,1)S(1)} %pad_add_fusion, bf16[4,64,16,64,1,1]{3,1,5,4,2,0:T(8,128)(2,1)S(1)} %bitcast.79, bf16[2,4,9,64,16,64]{5,4,3,2,1,0:T(8,128)(2,1)} %reshape.248), kind=kOutput, calls=%fused_computation.3 | convolution fusion | flops 618131456 | bytes 28852296 | tf_op jit(solution)/shard_map/while/body/eval_jaxpr/gqhd,sgjkhd->ghqsjk/dot_general | solution.py:88
  211.9 25.7 %fusion.1 = (f32[4,16,64]{2,1,0:T(8,128)S(1)}, bf16[4,16,64,2,9,64]{2,5,4,3,1,0:T(8,128)(2,1)}) fusion(f32[4,16,64,2,9,64]{2,5,4,3,1,0:T(8,128)} %get-tuple-element.38, f32[4,16,64]{2,1,0:T(8,128)S(1)} %get-tuple-element.37, pred[4,2,9]{2,1,0:T(4,128)(4,1)S(1)} %pad_add_fusion), kind=kLoop, calls=%fused_computation.4 | loop fusion | flops 23588864 | bytes 28344392 | tf_op jit(solution)/shard_map/while/body/eval_jaxpr/reduce_sum | solution.py:95
  237.6 0.0 copy-start.1
  237.6 17.5 %fusion.8 = bf16[4,64,16,64]{1,3,2,0:T(8,128)(2,1)} fusion(bf16[4,16,64,2,9,64]{2,5,4,3,1,0:T(8,128)(2,1)} %get-tuple-element.16, bf16[2,4,9,64,16,64]{5,4,3,2,1,0:T(8,128)(2,1)} %reshape.246, f32[4,64,16]{1,2,0:T(8,128)S(1)} %bitcast.81), kind=kOutput, calls=%fused_computation.17 | convolution fusion | flops 604504064 | bytes 19415040 | tf_op jit(solution)/shard_map/while/body/eval_jaxpr/ghqsjk,sgjkhd->gqhd/dot_general | solution.py:97
  255.1 1.9 copy.24
  257.1 1.5 reshape.249
  258.6 1.1 copy.25
  259.7 3.1 %fusion.33 = bf16[1,16,16,1024]{3,2,1,0:T(8,128)(2,1)} fusion(bf16[16,16,1024]{2,1,0:T(8,128)(2,1)S(1)} %bitcast.80, bf16[1024,1024]{1,0:T(8,128)(2,1)} %param.11), kind=kOutput, calls=%fused_computation.30 | convolution fusion | flops 537133056 | bytes 3145728 | tf_op jit(solution)/shard_map/dot_general | solution.py:113
  262.8 0.0 copy-done.1
  (9 shorter events, 0.1 us)
Async XLA Ops:
  0.0 1.6 copy-start
  6.0 25.9 %collective-permute-start = (bf16[16,16,2048]{2,1,0:T(8,128)(2,1)S(1)}, bf16[16,16,2048]{2,1,0:T(8,128)(2,1)S(1)}, u32[]{:S(2)}, u32[]{:S(2)}) collective-permute-start(bf16[16,16,2048]{2,1,0:T(8,128)(2,1)S(1)} %get-tuple-element.32), channel_id=1, source_target_pairs={{0,1},{1,2},{2,3},{4,5},{5,6},{6,7},{8,9},{9,10},{10,11},{12,13},{... | collective-permute-start | bytes 3145736 | tf_op jit(solution)/shard_map/ppermute | solution.py:32
  32.1 3.9 %collective-permute-start.1 = (bf16[2,16,8,2048]{3,2,1,0:T(8,128)(2,1)S(1)}, bf16[2,16,8,2048]{3,2,1,0:T(8,128)(2,1)S(1)}, u32[]{:S(2)}, u32[]{:S(2)}) collective-permute-start(bf16[2,16,8,2048]{3,2,1,0:T(8,128)(2,1)S(1)} %get-tuple-element.29), channel_id=1, source_target_pairs={{0,4},{4,0},{1,5},{5,1},{2,6},{6,2},{3,7},{7,3},{8,12},{12,8},{9,1... | collective-permute-start | bytes 3145736 | tf_op jit(solution)/shard_map/ppermute | solution.py:21
  33.7 14.6 %copy-start.5 = (s32[1,2,2,9]{3,2,1,0:T(2,128)S(1)}, s32[1,2,2,9]{3,2,1,0:T(2,128)}, u32[]{:S(2)}) copy-start(s32[1,2,2,9]{3,2,1,0:T(2,128)} %param.12) | copy-start | bytes 436
  33.7 15.3 %copy-start.7 = (s32[1,2,2]{2,1,0:T(2,128)S(1)}, s32[1,2,2]{2,1,0:T(2,128)}, u32[]{:S(2)}) copy-start(s32[1,2,2]{2,1,0:T(2,128)} %param.13) | copy-start | bytes 52
  33.7 15.3 %copy-start.6 = (bf16[1,16,16,1024]{3,2,1,0:T(8,128)(2,1)S(1)}, bf16[1,16,16,1024]{3,2,1,0:T(8,128)(2,1)}, u32[]{:S(2)}) copy-start(bf16[1,16,16,1024]{3,2,1,0:T(8,128)(2,1)} %param.7) | copy-start | bytes 1572868
  33.7 3.8 %collective-permute-start.2 = (bf16[2,16,8,2048]{3,2,1,0:T(8,128)(2,1)S(1)}, bf16[2,16,8,2048]{3,2,1,0:T(8,128)(2,1)S(1)}, u32[]{:S(2)}, u32[]{:S(2)}) collective-permute-start(bf16[2,16,8,2048]{3,2,1,0:T(8,128)(2,1)S(1)} %get-tuple-element.30), channel_id=1, source_target_pairs={{4,0},{0,4},{5,1},{1,5},{6,2},{2,6},{7,3},{3,7},{12,8},{8,12},{13,... | collective-permute-start | bytes 3145736 | tf_op jit(solution)/shard_map/ppermute | solution.py:24
  36.0 1.5 copy-start.2
  37.5 1.0 copy-start.3
  41.5 49.6 %collective-permute-start.3 = (bf16[2,8,32,2048]{3,2,1,0:T(8,128)(2,1)}, bf16[2,8,32,2048]{3,2,1,0:T(8,128)(2,1)}, u32[]{:S(2)}, u32[]{:S(2)}) collective-permute-start(bf16[2,8,32,2048]{3,2,1,0:T(8,128)(2,1)} %get-tuple-element.26), channel_id=1, source_target_pairs={{0,8},{8,16},{16,24},{24,32},{32,40},{40,48},{48,56},{56,64},{64,7... | collective-permute-start | bytes 6291464 | tf_op jit(solution)/shard_map/ppermute | solution.py:21
  46.1 52.1 %collective-permute-start.4 = (bf16[2,8,32,2048]{3,2,1,0:T(8,128)(2,1)}, bf16[2,8,32,2048]{3,2,1,0:T(8,128)(2,1)}, u32[]{:S(2)}, u32[]{:S(2)}) collective-permute-start(bf16[2,8,32,2048]{3,2,1,0:T(8,128)(2,1)} %get-tuple-element.28), channel_id=1, source_target_pairs={{8,0},{16,8},{24,16},{32,24},{40,32},{48,40},{56,48},{64,56},{72,6... | collective-permute-start | bytes 6291464 | tf_op jit(solution)/shard_map/ppermute | solution.py:24
  166.0 24.7 %copy-start.4 = (bf16[2,2,8,8,16,64]{5,3,2,4,1,0:T(8,128)(2,1)S(1)}, bf16[2,2,8,8,16,64]{5,3,2,4,1,0:T(8,128)(2,1)}, u32[]{:S(2)}) copy-start(bf16[2,2,8,8,16,64]{5,3,2,4,1,0:T(8,128)(2,1)} %copy.20) | copy-start | bytes 1572868
  237.6 25.2 %copy-start.1 = (bf16[1024,1024]{1,0:T(8,128)(2,1)S(1)}, bf16[1024,1024]{1,0:T(8,128)(2,1)}, u32[]{:S(2)}) copy-start(bf16[1024,1024]{1,0:T(8,128)(2,1)} %param.9) | copy-start | bytes 6291460
where the time goes:
time: 266 us; the launch traced here: 263 us
  local copies, waits for them, and re-layouts  89.6 us (34%)
  waiting for transfers between devices  69.1 us (26%)
  matrix products  49.1 us (18%)
  other arithmetic  43 us (16%)
  starting transfers between devices  11.7 us (4%)
    ppermute x2, waiting for transfers between devices, extended(): lax.ppermute(lax.slice_in_dim(block, block.shape[dim] - width, None, axis...  37.8 us
    reduce_sum x1, other arithmetic, attend(): denominator = jnp.sum(exponent, axis=(3, 4, 5))  25.7 us
    reshape x1, local copies, waits for them, and re-layouts, attend(): chosen[..., feature_dim:]  24.7 us
    reshape x1, local copies, waits for them, and re-layouts, attend(): chosen[..., :feature_dim]  24.7 us
    ppermute x1, waiting for transfers between devices, passed_along(): lax.ppermute(value, axis, [(source, source + steps) for source in range(i...  22.7 us
    dot_general x1, matrix products, attend(): jnp.einsum('gqhd,sgjkhd->ghqsjk', block_q, key_part, preferred_element_ty...  21.2 us
    dot_general x1, matrix products, attend(): jnp.einsum('ghqsjk,sgjkhd->gqhd', weights, value_part, preferred_element_...  17.5 us
    gather x1, local copies, waits for them, and re-layouts, attend(): chosen = jnp.take(tiled_pairs, block_tiles.reshape(-1), axis=1)  11.4 us
  transfers between devices with their start and end apart: 5, of which 5 were waited for; matrix products, arithmetic and copies ran while one was open for 3% of the time, Pallas kernels for 0%

commit v1 on v0

v1 whole, which is shorter than its diff:
```python
import functools

import jax
import jax.numpy as jnp
from jax import lax
from jax.experimental import pallas as pl
from jax.experimental.pallas import tpu as pltpu
from jax.sharding import PartitionSpec as P

HEADS = 16
HEAD = 64
TILE = 8
WIN = 9
D = 1024
HALF = D // 2
TOK = 128
NC = 4
CH = TOK // NC
VROWS = HEAD + 16
DEAD = -1e38
FLOOR = -1e30
MESH = pl.DeviceIdType.MESH
COMM = True
NT = (((1,), (1,)), ((), ()))
TN = (((0,), (0,)), ((), ()))


def kernel(
    x_ref, wq_ref, wk_ref, wv_ref, wo_ref, codes_ref, counts_ref, out_ref,
    xs, wq, wk, wv, wo, wvt, qz, ks, vt, os_, ms, bias, snd, full,
    w_sem, x_sem,
    p_ss, p_rs, y_ss, y_rs, n0_ss, n0_rs, n1_ss, n1_rs, f_ss, f_rs, b_ss, b_rs, a_ss, a_rs,
):
    f32, bf16 = jnp.float32, jnp.bfloat16
    lat, c, frame = lax.axis_index("lat"), lax.axis_index("lon"), lax.axis_index("frame")
    nlat, nframe = lax.axis_size("lat"), lax.axis_size("frame")
    o = 1 - c
    has_n, has_s = lat > 0, lat < nlat - 1
    has_prev, has_next = frame > 0, frame < nframe - 1

    cols = pl.ds(pl.multiple_of(c * HALF, HALF), HALF)
    x_copies = [pltpu.make_async_copy(x_ref.at[r], xs.at[0, 1 + r, c], x_sem.at[r]) for r in range(2)]
    w_copies = [
        pltpu.make_async_copy(wv_ref.at[:, cols], wv, w_sem.at[0]),
        pltpu.make_async_copy(wk_ref.at[:, cols], wk, w_sem.at[1]),
        pltpu.make_async_copy(wq_ref.at[:, cols], wq, w_sem.at[2]),
        pltpu.make_async_copy(wo_ref, wo, w_sem.at[3]),
    ]
    for copy in x_copies:
        copy.start()
    for copy in w_copies:
        copy.start()

    def remote(src, dst, ss, rs, dev):
        return pltpu.make_async_remote_copy(
            src_ref=src, dst_ref=dst, send_sem=ss, recv_sem=rs, device_id=dev, device_id_type=MESH
        )

    def part(i):
        return pl.ds(pl.multiple_of(i * CH, CH), CH)

    def own_to_peer(r, lon):
        return remote(x_ref.at[r], xs.at[0, 1 + r, lon], p_ss.at[r], p_rs.at[r], {"lon": o})

    def to_next(r, i):
        k = r * NC + i
        return remote(x_ref.at[r, part(i)], xs.at[1, 1 + r, c, part(i)], y_ss.at[k], y_rs.at[k], {"frame": frame + 1})

    def side_dev(side):
        return {"lat": lat - 1 if side == 0 else lat + 1}

    def own_to_side(side, i):
        k = side * NC + i
        return remote(
            x_ref.at[side, part(i)], xs.at[0, 3 - 3 * side, c, part(i)], n0_ss.at[k], n0_rs.at[k], side_dev(side)
        )

    def prev_to_side(side, i):
        k = side * NC + i
        return remote(
            xs.at[1, 1 + side, c, part(i)], xs.at[1, 3 - 3 * side, c, part(i)], n1_ss.at[k], n1_rs.at[k], side_dev(side)
        )

    def forward(fr, row, i, lon):
        k = (fr * 4 + row) * NC + i
        block = xs.at[fr, row, lon, part(i)]
        return remote(block, block, f_ss.at[k], f_rs.at[k], {"lon": o})

    def bias_to_peer(lon):
        return remote(bias.at[lon], bias.at[lon], b_ss.at[0], b_rs.at[0], {"lon": o})

    def att_to_peer(r, lon):
        return remote(snd.at[r], full.at[r, lon], a_ss.at[r], a_rs.at[r], {"lon": o})

    send_to = (has_n, has_s)
    gets_from = (has_s, has_n)

    if COMM:
        barrier = pltpu.get_barrier_semaphore()

        def greet(dev):
            pl.semaphore_signal(barrier, inc=1, device_id=dev, device_id_type=MESH)

        greet({"lon": o})
        pl.when(has_n)(lambda: greet({"lat": lat - 1}))
        pl.when(has_s)(lambda: greet({"lat": lat + 1}))
        pl.when(has_prev)(lambda: greet({"frame": frame - 1}))
        pl.when(has_next)(lambda: greet({"frame": frame + 1}))

    ri = lax.broadcasted_iota(jnp.int32, (8, TOK), 0)
    li = lax.broadcasted_iota(jnp.int32, (8, TOK), 1)
    second = (li // TILE) % 2 == 1
    gcol = 2 * c + (li // TILE) % 2
    wcol = (ri - gcol + 5) % 4
    first_ext = []
    outer = [jnp.where(has_n, 0, 3), jnp.where(has_s, 3, 0)]
    for r in range(2):
        first = jnp.minimum(jnp.maximum(2 * lat + r - 1, 0), 2 * nlat - 3) - 2 * lat + 1
        first_ext.append(first)
        cnt = jnp.where(second, counts_ref[0, r, 1], counts_ref[0, r, 0])
        for slot in range(3):
            ext = outer[r] if slot == 0 else slot
            want = jnp.where(jnp.logical_and(wcol < 3, ri < 4), 3 * (ext - first) + wcol, -1)
            live = jnp.zeros((8, TOK), f32)
            for j in range(WIN):
                code = jnp.where(second, codes_ref[0, r, 1, j], codes_ref[0, r, 0, j])
                hit = jnp.logical_and(code == want, j < cnt)
                live = jnp.where(hit, 1.0, live)
            bias[c, r, slot] = jnp.where(live > 0.5, 0.0, DEAD)
    vt[:, :, :, HEAD:, :] = jnp.ones((2, 4, 8, VROWS - HEAD, 2 * TOK), bf16)

    if COMM:
        greeted = (
            1
            + has_n.astype(jnp.int32)
            + has_s.astype(jnp.int32)
            + has_prev.astype(jnp.int32)
            + has_next.astype(jnp.int32)
        )
        pl.semaphore_wait(barrier, greeted)
        for r in range(2):
            own_to_peer(r, c).start()

        @pl.when(has_next)
        def _():
            for i in range(NC):
                to_next(0, i).start()

        for side in range(2):

            @pl.when(send_to[side])
            def _(side=side):
                for i in range(NC):
                    own_to_side(side, i).start()

        @pl.when(has_next)
        def _():
            for i in range(NC):
                to_next(1, i).start()

        bias_to_peer(c).start()

    def pump_own_sides(i):
        for side in range(2):

            @pl.when(gets_from[side])
            def _(side=side):
                own_to_side(side, i).wait_recv()
                forward(0, 3 - 3 * side, i, c).start()

    def pump_prev(r, i):
        @pl.when(has_prev)
        def _():
            to_next(r, i).wait_recv()

            @pl.when(send_to[r])
            def _():
                prev_to_side(r, i).start()

            forward(1, 1 + r, i, c).start()

    def pump_prev_side(side, i):
        @pl.when(jnp.logical_and(has_prev, gets_from[side]))
        def _():
            prev_to_side(side, i).wait_recv()
            forward(1, 3 - 3 * side, i, c).start()

    def project(fr, row):
        x = xs[fr, row].reshape(2 * TOK, D)
        key = jnp.dot(x, wk[...], preferred_element_type=f32).astype(bf16)
        for pair in range(4):
            ks[fr, row, pair] = key[:, pair * 128 : (pair + 1) * 128]
        value = lax.dot_general(wvt[...], x, NT, preferred_element_type=f32).astype(bf16)
        vt[fr, row, :, :HEAD, :] = value.reshape(8, HEAD, 2 * TOK)

    def attend(fr, rows_slots, r, pair, first):
        for j in range(2):
            h = 2 * pair + j
            q = qz[r, h]
            parts = []
            best = None
            for row, slot in rows_slots:
                s = lax.dot_general(ks[fr, row, pair], q, NT, preferred_element_type=f32)
                s = s.reshape(2, TILE, 2, TILE, 2 * TOK)
                b = jnp.concatenate([bias[0, r, slot], bias[1, r, slot]], axis=1)[:4]
                b = b.reshape(2, 2, 1, 2 * TOK)
                top = jnp.max(s, axis=1) + b
                top = jnp.max(jnp.max(top, axis=0), axis=0)
                best = top if best is None else jnp.maximum(best, top)
                parts.append((s, b, row))
            m = jnp.maximum(jnp.max(best, axis=0, keepdims=True), FLOOR)
            if not first:
                m_old = ms[r, h, :1]
                m = jnp.maximum(m, m_old)
            total = None
            for s, b, row in parts:
                p = jnp.exp(s + (b - m)[:, None]).reshape(2 * TOK, 2 * TOK).astype(bf16)
                t = jnp.dot(vt[fr, row, h], p, preferred_element_type=f32)
                total = t if total is None else total + t
            if not first:
                total = total + os_[r, h] * jnp.exp(m_old - m)
            os_[r, h] = total
            ms[r, h] = jnp.broadcast_to(m, (8, 2 * TOK))

    w_copies[0].wait()
    wvt[...] = wv[...].T
    for copy in x_copies:
        copy.wait()
    if COMM:
        for r in range(2):
            own_to_peer(r, o).wait_recv()
        bias_to_peer(o).wait_recv()
    w_copies[1].wait()
    w_copies[2].wait()
    low = lax.broadcasted_iota(jnp.int32, (2 * TOK, 128), 1) < HEAD

    @pl.loop(0, 2)
    def _(r):
        project(0, 1 + r)
        x = xs[0, 1 + r].reshape(2 * TOK, D)
        query = jnp.dot(x, wq[...], preferred_element_type=f32).astype(bf16).astype(f32) * 0.125
        for pair in range(4):
            q = query[:, pair * 128 : (pair + 1) * 128]
            qz[r, 2 * pair] = jnp.where(low, q, 0.0).astype(bf16)
            qz[r, 2 * pair + 1] = jnp.where(low, 0.0, q).astype(bf16)

    @pl.loop(0, 4)
    def _(g):
        for u in range(2):
            attend(0, [(1, 1), (2, 2)], g // 2, (g % 2) * 2 + u, True)
        if COMM:
            pump_own_sides(g)
            pump_prev(0, g)

    for side in range(2):

        @pl.when(gets_from[side])
        def _(side=side):
            if COMM:
                for i in range(NC):
                    forward(0, 3 - 3 * side, i, o).wait_recv()
            project(0, 3 - 3 * side)

    @pl.loop(0, 4)
    def _(g):
        r = g // 2
        row = jnp.where(r == 0, outer[0], outer[1])
        for u in range(2):
            attend(0, [(row, 0)], r, (g % 2) * 2 + u, False)
        if COMM:
            pump_prev(1, g)

    @pl.when(has_prev)
    def _():
        @pl.loop(0, 2)
        def _(r0):
            row = 1 + r0
            if COMM:
                for i in range(NC):
                    forward(1, row, i, o).wait_recv()
            project(1, row)

            @pl.loop(0, 8)
            def _(g):
                attend(1, [(row, row)], g // 4, g % 4, False)

        for side in range(2):

            @pl.when(gets_from[side])
            def _(side=side):
                if COMM:
                    for i in range(NC):
                        pump_prev_side(side, i)
                    for i in range(NC):
                        forward(1, 3 - 3 * side, i, o).wait_recv()
                project(1, 3 - 3 * side)

        @pl.loop(0, 8)
        def _(g):
            r = g // 4
            row = jnp.where(r == 0, outer[0], outer[1])
            attend(1, [(row, 0)], r, g % 4, False)

    w_copies[3].wait()
    for r in range(2):
        for h in range(8):
            total = os_[r, h]
            att = (total[:HEAD] * (1.0 / total[HEAD : HEAD + 1])).astype(bf16)
            rows = pl.ds(h * HEAD, HEAD)
            mine_first = c == 0
            full[r, c, rows] = jnp.where(mine_first, att[:, :TOK], att[:, TOK:])
            snd[r, rows] = jnp.where(mine_first, att[:, TOK:], att[:, :TOK])
        if COMM:
            att_to_peer(r, c).start()
    for r in range(2):
        if COMM:
            att_to_peer(r, o).wait_recv()
        a = full[r].reshape(D, TOK)
        out_ref[r] = lax.dot_general(a, wo[...], TN, preferred_element_type=f32).astype(bf16)

    if COMM:
        for r in range(2):
            own_to_peer(r, c).wait_send()
            att_to_peer(r, c).wait_send()
        bias_to_peer(c).wait_send()

        @pl.when(has_next)
        def _():
            for r in range(2):
                for i in range(NC):
                    to_next(r, i).wait_send()

        for side in range(2):

            @pl.when(send_to[side])
            def _(side=side):
                for i in range(NC):
                    own_to_side(side, i).wait_send()

            @pl.when(gets_from[side])
            def _(side=side):
                for i in range(NC):
                    forward(0, 3 - 3 * side, i, c).wait_send()

        @pl.when(has_prev)
        def _():
            for side in range(2):
                for i in range(NC):
                    forward(1, 1 + side, i, c).wait_send()

                @pl.when(send_to[side])
                def _(side=side):
                    for i in range(NC):
                        prev_to_side(side, i).wait_send()

                @pl.when(gets_from[side])
                def _(side=side):
                    for i in range(NC):
                        forward(1, 3 - 3 * side, i, c).wait_send()


def on_device(frames_in, w_query, w_key, w_value, w_out, codes, counts):
    shape = frames_in.shape
    x = frames_in.reshape(2, TOK, D)
    bf16, f32 = jnp.bfloat16, jnp.float32
    dma = pltpu.SemaphoreType.DMA
    anywhere = pl.BlockSpec(memory_space=pl.ANY)
    scalars = pl.BlockSpec(memory_space=pltpu.SMEM)
    out = pl.pallas_call(
        kernel,
        out_shape=jax.ShapeDtypeStruct((2, TOK, D), bf16),
        in_specs=[anywhere] * 5 + [scalars] * 2,
        out_specs=pl.BlockSpec(memory_space=pltpu.VMEM),
        scratch_shapes=[
            pltpu.VMEM((2, 4, 2, TOK, D), bf16),
            pltpu.VMEM((D, HALF), bf16),
            pltpu.VMEM((D, HALF), bf16),
            pltpu.VMEM((D, HALF), bf16),
            pltpu.VMEM((D, D), bf16),
            pltpu.VMEM((HALF, D), bf16),
            pltpu.VMEM((2, 8, 2 * TOK, 128), bf16),
            pltpu.VMEM((2, 4, 4, 2 * TOK, 128), bf16),
            pltpu.VMEM((2, 4, 8, VROWS, 2 * TOK), bf16),
            pltpu.VMEM((2, 8, VROWS, 2 * TOK), f32),
            pltpu.VMEM((2, 8, 8, 2 * TOK), f32),
            pltpu.VMEM((2, 2, 3, 8, TOK), f32),
            pltpu.VMEM((2, HALF, TOK), bf16),
            pltpu.VMEM((2, 2, HALF, TOK), bf16),
            dma((4,)),
            dma((2,)),
            dma((2,)),
            dma((2,)),
            dma((2 * NC,)),
            dma((2 * NC,)),
            dma((2 * NC,)),
            dma((2 * NC,)),
            dma((2 * NC,)),
            dma((2 * NC,)),
            dma((8 * NC,)),
            dma((8 * NC,)),
            dma((1,)),
            dma((1,)),
            dma((2,)),
            dma((2,)),
        ],
        compiler_params=pltpu.CompilerParams(
            vmem_limit_bytes=50 << 20,
            **(dict(collective_id=0, has_side_effects=True) if COMM else {}),
        ),
        cost_estimate=pl.CostEstimate(flops=12 * 10**9, bytes_accessed=8 << 20, transcendentals=6 << 20),
    )(x, w_query, w_key, w_value, w_out, codes, counts)
    return out.reshape(shape)


def solution(mesh):
    placed = (
        P("frame", "lat", "lon", None),
        P(),
        P(),
        P(),
        P(),
        P("frame", "lat", "lon", None),
        P("frame", "lat", "lon"),
    )
    return jax.shard_map(
        on_device,
        mesh=mesh,
        in_specs=placed,
        out_specs=P("frame", "lat", "lon", None),
        check_vma=False,
    )
```

time: 266 us -> 52 us (0.20); the launches traced: 263 us -> 51.6 us
  local copies, waits for them, and re-layouts: 89.6 us -> 4.79 us
  waiting for transfers between devices: 69.1 us -> 0 us
  matrix products: 49.1 us -> 0 us
  Pallas kernels: 0 us -> 46.8 us
  other arithmetic: 43 us -> 0 us
  starting transfers between devices: 11.7 us -> 0 us
    ppermute x5 -> x0, waiting for transfers between devices: 69.1 us -> none  [the longest x2 37.8 us: extended(): lax.ppermute(lax.slice_in_dim(block, block.shape[dim] - width, None, axis...]
    reshape x5 -> x0, local copies, waits for them, and re-layouts: 61.1 us -> none  [the longest x1 24.7 us: attend(): chosen[..., feature_dim:]]
    dot_general x6 -> x0, matrix products: 49.1 us -> none  [the longest x1 21.2 us: attend(): jnp.einsum('gqhd,sgjkhd->ghqsjk', block_q, key_part, preferred_element_ty...]
    pallas_call x0 -> x1, Pallas kernels: none -> 46.8 us  [on_device(): pl.pallas_call(kernel, out_shape=jax.ShapeDtypeStruct((2, TOK, D), bf16),...]
    reduce_sum x1 -> x0, other arithmetic: 25.7 us -> none  [attend(): denominator = jnp.sum(exponent, axis=(3, 4, 5))]
    ppermute x5 -> x0, starting transfers between devices: 11.7 us -> none  [the longest x2 6.29 us: extended(): lax.ppermute(lax.slice_in_dim(block, block.shape[dim] - width, None, axis...]
    gather x1 -> x0, local copies, waits for them, and re-layouts: 11.4 us -> none  [attend(): chosen = jnp.take(tiled_pairs, block_tiles.reshape(-1), axis=1)]
    select_n x2 -> x0, other arithmetic: 9.77 us -> none  [attend(): chosen = jnp.take(tiled_pairs, block_tiles.reshape(-1), axis=1)]
  transfers between devices with their start and end apart: 5 -> 0, of which waited for: 5 -> 0; matrix products, arithmetic and copies ran while one was open for 3% -> 0% of each run, Pallas kernels for 0% -> 0%
where the time goes in v1:
time: 52 us; the launch traced here: 51.6 us
  Pallas kernels  46.8 us (90%)
  local copies, waits for them, and re-layouts  4.79 us (9%)
    pallas_call x1, Pallas kernels, on_device(): pl.pallas_call(kernel, out_shape=jax.ShapeDtypeStruct((2, TOK, D), bf16),...  46.8 us
    unnamed x9, local copies, waits for them, and re-layouts  4.79 us

profile of v1, /device:TPU:111, one launch (start us, length us, event | category | flops | bytes accessed | tf_op | source)
XLA Modules:
  0.0 51.6 jit_solution(17946422886588697662)
XLA Ops:
  0.0 0.0 copy-start
  0.0 1.6 %copy-done = bf16[1024,1024]{1,0:T(8,128)(2,1)S(1)} copy-done((bf16[1024,1024]{1,0:T(8,128)(2,1)S(1)}, bf16[1024,1024]{1,0:T(8,128)(2,1)}, u32[]{:S(2)}) %copy-start) | copy-done | bytes 2097176
  1.6 0.0 copy-start.1
  1.6 1.0 %copy-done.1 = bf16[1,16,16,1024]{3,2,1,0:T(8,128)(2,1)S(1)} copy-done((bf16[1,16,16,1024]{3,2,1,0:T(8,128)(2,1)S(1)}, bf16[1,16,16,1024]{3,2,1,0:T(8,128)(2,1)}, u32[]{:S(2)}) %copy-start.1) | copy-done | bytes 524312
  2.6 0.0 copy-start.2
  2.6 0.7 %copy-done.2 = s32[1,2,2,9]{3,2,1,0:T(2,128)S(1)} copy-done((s32[1,2,2,9]{3,2,1,0:T(2,128)S(1)}, s32[1,2,2,9]{3,2,1,0:T(2,128)}, u32[]{:S(2)}) %copy-start.2) | copy-done | bytes 168
  3.3 0.0 copy-start.3
  3.3 0.7 %copy-done.3 = s32[1,2,2]{2,1,0:T(2,128)S(1)} copy-done((s32[1,2,2]{2,1,0:T(2,128)S(1)}, s32[1,2,2]{2,1,0:T(2,128)}, u32[]{:S(2)}) %copy-start.3) | copy-done | bytes 40
  4.0 46.8 %shard_map.73 = bf16[2,128,1024]{2,1,0:T(8,128)(2,1)S(1)} custom-call(bf16[2,128,1024]{2,1,0:T(8,128)(2,1)S(1)} %bitcast.3, bf16[1024,1024]{1,0:T(8,128)(2,1)S(1)} %copy-done, bf16[1024,1024]{1,0:T(8,128)(2,1)} %wk_ref.1, bf16[1024,1024]{1,0:T(8,128)(2,1)} %wv_ref.1, bf16[1024,1024]{1,0:T(8,128)(2,1)} %wo_ref.1, s32[1,2,2,9]{3,2,1,0:T(2,128)S(1)} %copy-done.2, ...), custom_call_target="tpu_custom_call" | custom-call | flops 12000000000 | bytes 8388608 | tf_op jit(solution)/shard_map/pallas_call | solution.py:369
  50.8 0.8 %copy.9 = bf16[1,16,16,1024]{3,2,1,0:T(8,128)(2,1)} copy(bf16[1,16,16,1024]{3,2,1,0:T(8,128)(2,1)S(1)} %bitcast.2) | data formatting | bytes 1048576
Async XLA Ops:
  0.0 1.6 %copy-start = (bf16[1024,1024]{1,0:T(8,128)(2,1)S(1)}, bf16[1024,1024]{1,0:T(8,128)(2,1)}, u32[]{:S(2)}) copy-start(bf16[1024,1024]{1,0:T(8,128)(2,1)} %wq_ref.1) | copy-start | bytes 6291460
  1.6 1.0 %copy-start.1 = (bf16[1,16,16,1024]{3,2,1,0:T(8,128)(2,1)S(1)}, bf16[1,16,16,1024]{3,2,1,0:T(8,128)(2,1)}, u32[]{:S(2)}) copy-start(bf16[1,16,16,1024]{3,2,1,0:T(8,128)(2,1)} %param.7) | copy-start | bytes 1572868
  2.6 0.7 %copy-start.2 = (s32[1,2,2,9]{3,2,1,0:T(2,128)S(1)}, s32[1,2,2,9]{3,2,1,0:T(2,128)}, u32[]{:S(2)}) copy-start(s32[1,2,2,9]{3,2,1,0:T(2,128)} %codes_ref.1) | copy-start | bytes 436
  3.3 0.7 %copy-start.3 = (s32[1,2,2]{2,1,0:T(2,128)S(1)}, s32[1,2,2]{2,1,0:T(2,128)}, u32[]{:S(2)}) copy-start(s32[1,2,2]{2,1,0:T(2,128)} %counts_ref.1) | copy-start | bytes 52

commit v2 on v1

--- a/solution.py
+++ b/solution.py
@@ -28,6 +28,7 @@
 def kernel(
     x_ref, wq_ref, wk_ref, wv_ref, wo_ref, codes_ref, counts_ref, out_ref,
     xs, wq, wk, wv, wo, wvt, qz, ks, vt, os_, ms, bias, snd, full,
+    s0, s1, s2, s3, s4, s5, s6, s7,
     w_sem, x_sem,
     p_ss, p_rs, y_ss, y_rs, n0_ss, n0_rs, n1_ss, n1_rs, f_ss, f_rs, b_ss, b_rs, a_ss, a_rs,
 ):
@@ -35,6 +36,7 @@
     lat, c, frame = lax.axis_index("lat"), lax.axis_index("lon"), lax.axis_index("frame")
     nlat, nframe = lax.axis_size("lat"), lax.axis_size("frame")
     o = 1 - c
+    ss = (s0, s1, s2, s3, s4, s5, s6, s7)
     has_n, has_s = lat > 0, lat < nlat - 1
     has_prev, has_next = frame > 0, frame < nframe - 1
 
@@ -67,7 +69,7 @@
         return remote(x_ref.at[r, part(i)], xs.at[1, 1 + r, c, part(i)], y_ss.at[k], y_rs.at[k], {"frame": frame + 1})
 
     def side_dev(side):
-        return {"lat": lat - 1 if side == 0 else lat + 1}
+        return {"lat": lat - 1 + 2 * side}
 
     def own_to_side(side, i):
         k = side * NC + i
@@ -128,6 +130,8 @@
                 live = jnp.where(hit, 1.0, live)
             bias[c, r, slot] = jnp.where(live > 0.5, 0.0, DEAD)
     vt[:, :, :, HEAD:, :] = jnp.ones((2, 4, 8, VROWS - HEAD, 2 * TOK), bf16)
+    w_copies[0].wait()
+    wvt[...] = wv[...].T
 
     if COMM:
         greeted = (
@@ -180,139 +184,167 @@
             forward(1, 1 + r, i, c).start()
 
     def pump_prev_side(side, i):
-        @pl.when(jnp.logical_and(has_prev, gets_from[side]))
-        def _():
-            prev_to_side(side, i).wait_recv()
-            forward(1, 3 - 3 * side, i, c).start()
-
-    def project(fr, row):
-        x = xs[fr, row].reshape(2 * TOK, D)
+        prev_to_side(side, i).wait_recv()
+        forward(1, 3 - 3 * side, i, c).start()
+
+    def project(x, fr, blk):
         key = jnp.dot(x, wk[...], preferred_element_type=f32).astype(bf16)
         for pair in range(4):
-            ks[fr, row, pair] = key[:, pair * 128 : (pair + 1) * 128]
+            ks[fr, blk, pair] = key[:, pair * 128 : (pair + 1) * 128]
         value = lax.dot_general(wvt[...], x, NT, preferred_element_type=f32).astype(bf16)
-        vt[fr, row, :, :HEAD, :] = value.reshape(8, HEAD, 2 * TOK)
-
-    def attend(fr, rows_slots, r, pair, first):
-        for j in range(2):
-            h = 2 * pair + j
-            q = qz[r, h]
-            parts = []
+        vt[fr, blk, :, :HEAD, :] = value.reshape(8, HEAD, 2 * TOK)
+
+    def row_of(fr, row):
+        return xs[fr, row].reshape(2 * TOK, D)
+
+    def attend(fr, blocks, r, first, group, ahead):
+        n = len(blocks)
+        masks = []
+        for _, (a, b) in blocks:
+            rows = [jnp.concatenate([bias[0, r, slot], bias[1, r, slot]], axis=1)[k : k + 2] for slot, k in (a, b)]
+            masks.append([v.reshape(2, 1, 2 * TOK) for v in rows])
+
+        def scores(h):
             best = None
-            for row, slot in rows_slots:
-                s = lax.dot_general(ks[fr, row, pair], q, NT, preferred_element_type=f32)
+            for k, (blk, _) in enumerate(blocks):
+                s = lax.dot_general(ks[fr, blk, h // 2], qz[r, h], NT, preferred_element_type=f32)
+                ss[(h * n + k) % 8][...] = s
                 s = s.reshape(2, TILE, 2, TILE, 2 * TOK)
-                b = jnp.concatenate([bias[0, r, slot], bias[1, r, slot]], axis=1)[:4]
-                b = b.reshape(2, 2, 1, 2 * TOK)
-                top = jnp.max(s, axis=1) + b
-                top = jnp.max(jnp.max(top, axis=0), axis=0)
-                best = top if best is None else jnp.maximum(best, top)
-                parts.append((s, b, row))
+                for u in range(2):
+                    top = jnp.max(jnp.max(s[u], axis=0) + masks[k][u], axis=0)
+                    best = top if best is None else jnp.maximum(best, top)
             m = jnp.maximum(jnp.max(best, axis=0, keepdims=True), FLOOR)
-            if not first:
-                m_old = ms[r, h, :1]
-                m = jnp.maximum(m, m_old)
+            if first:
+                return m, None
+            m_old = ms[r, h, :1]
+            return jnp.maximum(m, m_old), m_old
+
+        def values(h, m, m_old):
             total = None
-            for s, b, row in parts:
-                p = jnp.exp(s + (b - m)[:, None]).reshape(2 * TOK, 2 * TOK).astype(bf16)
-                t = jnp.dot(vt[fr, row, h], p, preferred_element_type=f32)
+            for k, (blk, _) in enumerate(blocks):
+                s = ss[(h * n + k) % 8][...].reshape(2, TILE, 2, TILE, 2 * TOK)
+                p = [jnp.exp(s[u] + (masks[k][u] - m)[None]).reshape(TOK, 2 * TOK).astype(bf16) for u in range(2)]
+                t = jnp.dot(vt[fr, blk, h], jnp.concatenate(p, axis=0), preferred_element_type=f32)
                 total = t if total is None else total + t
             if not first:
                 total = total + os_[r, h] * jnp.exp(m_old - m)
             os_[r, h] = total
             ms[r, h] = jnp.broadcast_to(m, (8, 2 * TOK))
 
-    w_copies[0].wait()
-    wvt[...] = wv[...].T
+        steps = 8 // group
+        state = {}
+        for g in range(steps + ahead):
+            if g < steps:
+                for h in range(g * group, (g + 1) * group):
+                    state[h] = scores(h)
+            if g >= ahead:
+                for h in range((g - ahead) * group, (g - ahead + 1) * group):
+                    values(h, *state.pop(h))
+
+    low = lax.broadcasted_iota(jnp.int32, (TOK, 128), 1) < HEAD
     for copy in x_copies:
         copy.wait()
-    if COMM:
-        for r in range(2):
-            own_to_peer(r, o).wait_recv()
-        bias_to_peer(o).wait_recv()
     w_copies[1].wait()
     w_copies[2].wait()
-    low = lax.broadcasted_iota(jnp.int32, (2 * TOK, 128), 1) < HEAD
+
+    @pl.loop(0, 2)
+    def _(t):
+        lon = jnp.where(t == 0, c, o)
+
+        @pl.when(t == 1)
+        def _():
+            if COMM:
+                for r in range(2):
+                    own_to_peer(r, o).wait_recv()
+                bias_to_peer(o).wait_recv()
+
+        x = jnp.concatenate([xs[0, 1, lon], xs[0, 2, lon]], axis=0)
+        project(x, 0, 1 + lon)
+        query = jnp.dot(x, wq[...], preferred_element_type=f32).astype(bf16).astype(f32) * 0.125
+        place = pl.ds(pl.multiple_of(lon * TOK, TOK), TOK)
+        for r in range(2):
+            for pair in range(4):
+                q = query[r * TOK : (r + 1) * TOK, pair * 128 : (pair + 1) * 128]
+                qz[r, 2 * pair, place] = jnp.where(low, q, 0.0).astype(bf16)
+                qz[r, 2 * pair + 1, place] = jnp.where(low, 0.0, q).astype(bf16)
 
     @pl.loop(0, 2)
     def _(r):
-        project(0, 1 + r)
-        x = xs[0, 1 + r].reshape(2 * TOK, D)
-        query = jnp.dot(x, wq[...], preferred_element_type=f32).astype(bf16).astype(f32) * 0.125
-        for pair in range(4):
-            q = query[:, pair * 128 : (pair + 1) * 128]
-            qz[r, 2 * pair] = jnp.where(low, q, 0.0).astype(bf16)
-            qz[r, 2 * pair + 1] = jnp.where(low, 0.0, q).astype(bf16)
-
-    @pl.loop(0, 4)
-    def _(g):
-        for u in range(2):
-            attend(0, [(1, 1), (2, 2)], g // 2, (g % 2) * 2 + u, True)
         if COMM:
-            pump_own_sides(g)
-            pump_prev(0, g)
-
-    for side in range(2):
-
-        @pl.when(gets_from[side])
-        def _(side=side):
+            for i in range(2):
+                pump_own_sides(2 * r + i)
+                pump_prev(0, 2 * r + i)
+        attend(0, [(1, ((1, 0), (2, 0))), (2, ((1, 2), (2, 2)))], r, True, 2, 1)
+
+    @pl.loop(0, 2)
+    def _(side):
+        @pl.when(jnp.where(side == 0, has_s, has_n))
+        def _():
+            row = 3 - 3 * side
             if COMM:
                 for i in range(NC):
-                    forward(0, 3 - 3 * side, i, o).wait_recv()
-            project(0, 3 - 3 * side)
-
-    @pl.loop(0, 4)
-    def _(g):
-        r = g // 2
+                    forward(0, row, i, o).wait_recv()
+            project(row_of(0, row), 0, row)
+
+    @pl.loop(0, 2)
+    def _(r):
+        if COMM:
+            pump_prev(1, 2 * r)
+            pump_prev(1, 2 * r + 1)
         row = jnp.where(r == 0, outer[0], outer[1])
-        for u in range(2):
-            attend(0, [(row, 0)], r, (g % 2) * 2 + u, False)
-        if COMM:
-            pump_prev(1, g)
+        attend(0, [(row, ((0, 0), (0, 2)))], r, False, 4, 1)
 
     @pl.when(has_prev)
     def _():
         @pl.loop(0, 2)
-        def _(r0):
-            row = 1 + r0
+        def _(t):
+            row = 1 + t
             if COMM:
                 for i in range(NC):
                     forward(1, row, i, o).wait_recv()
-            project(1, row)
-
-            @pl.loop(0, 8)
-            def _(g):
-                attend(1, [(row, row)], g // 4, g % 4, False)
-
-        for side in range(2):
-
-            @pl.when(gets_from[side])
-            def _(side=side):
+            project(row_of(1, row), 1, row)
+
+            @pl.loop(0, 2)
+            def _(r):
+                attend(1, [(row, ((row, 0), (row, 2)))], r, False, 4, 1)
+
+    mine_first = c == 0
+
+    @pl.loop(0, 2)
+    def _(t):
+        r = 1 - t
+
+        @pl.when(has_prev)
+        def _():
+            row = jnp.where(jnp.logical_and(t == 0, has_s), 3, 0)
+
+            @pl.when(jnp.logical_or(t == 0, jnp.logical_and(has_n, has_s)))
+            def _():
                 if COMM:
+                    side = jnp.where(row == 3, 0, 1)
                     for i in range(NC):
                         pump_prev_side(side, i)
                     for i in range(NC):
-                        forward(1, 3 - 3 * side, i, o).wait_recv()
-                project(1, 3 - 3 * side)
-
-        @pl.loop(0, 8)
-        def _(g):
-            r = g // 4
-            row = jnp.where(r == 0, outer[0], outer[1])
-            attend(1, [(row, 0)], r, g % 4, False)
-
-    w_copies[3].wait()
-    for r in range(2):
+                        forward(1, row, i, o).wait_recv()
+                project(row_of(1, row), 1, row)
+
+            mask_row = jnp.where(r == 0, outer[0], outer[1])
+            attend(1, [(mask_row, ((0, 0), (0, 2)))], r, False, 4, 1)
+
         for h in range(8):
             total = os_[r, h]
             att = (total[:HEAD] * (1.0 / total[HEAD : HEAD + 1])).astype(bf16)
             rows = pl.ds(h * HEAD, HEAD)
-            mine_first = c == 0
             full[r, c, rows] = jnp.where(mine_first, att[:, :TOK], att[:, TOK:])
             snd[r, rows] = jnp.where(mine_first, att[:, TOK:], att[:, :TOK])
         if COMM:
             att_to_peer(r, c).start()
-    for r in range(2):
+
+    w_copies[3].wait()
+
+    @pl.loop(0, 2)
+    def _(t):
+        r = 1 - t
         if COMM:
             att_to_peer(r, o).wait_recv()
         a = full[r].reshape(D, TOK)
@@ -386,6 +418,7 @@
             pltpu.VMEM((2, 2, 3, 8, TOK), f32),
             pltpu.VMEM((2, HALF, TOK), bf16),
             pltpu.VMEM((2, 2, HALF, TOK), bf16),
+            *([pltpu.VMEM((2 * TOK, 2 * TOK), f32)] * 8),
             dma((4,)),
             dma((2,)),
             dma((2,)),
@@ -404,7 +437,7 @@
             dma((2,)),
         ],
         compiler_params=pltpu.CompilerParams(
-            vmem_limit_bytes=50 << 20,
+            vmem_limit_bytes=60 << 20,
             **(dict(collective_id=0, has_side_effects=True) if COMM else {}),
         ),
         cost_estimate=pl.CostEstimate(flops=12 * 10**9, bytes_accessed=8 << 20, transcendentals=6 << 20),

time: 52 us -> 34.6 us (0.67)
  Pallas kernels: 46.8 us -> 32.6 us
  local copies, waits for them, and re-layouts: 4.79 us -> 1.88 us
    pallas_call x1, Pallas kernels: 46.8 us -> 32.6 us  [on_device(): pl.pallas_call(kernel, out_shape=jax.ShapeDtypeStruct((2, TOK, D), bf16),...]
    unnamed x9 -> x1, local copies, waits for them, and re-layouts: 4.79 us -> 1.88 us
where the time goes in v2:
time: 34.6 us; the launch traced here: 34.5 us
  Pallas kernels  32.6 us (94%)
  local copies, waits for them, and re-layouts  1.88 us (5%)
    pallas_call x1, Pallas kernels, on_device(): pl.pallas_call(kernel, out_shape=jax.ShapeDtypeStruct((2, TOK, D), bf16),...  32.6 us
    unnamed x1, local copies, waits for them, and re-layouts  1.88 us

profile of v2, /device:TPU:111, one launch (start us, length us, event | category | flops | bytes accessed | tf_op | source)
XLA Modules:
  0.0 34.5 jit_solution(5095309837617858005)
XLA Ops:
  0.0 32.6 %shard_map.73 = bf16[2,128,1024]{2,1,0:T(8,128)(2,1)} custom-call(bf16[2,128,1024]{2,1,0:T(8,128)(2,1)} %bitcast.3, bf16[1024,1024]{1,0:T(8,128)(2,1)} %wq_ref.1, bf16[1024,1024]{1,0:T(8,128)(2,1)} %wk_ref.1, bf16[1024,1024]{1,0:T(8,128)(2,1)} %wv_ref.1, bf16[1024,1024]{1,0:T(8,128)(2,1)} %wo_ref.1, s32[1,2,2,9]{3,2,1,0:T(2,128)} %codes_ref.1, ...), custom_call_target="tpu_custom_call" | custom-call | flops 12000000000 | bytes 8388608 | tf_op jit(solution)/shard_map/pallas_call | solution.py:401
  32.6 1.9 %copy.9 = bf16[1,16,16,1024]{3,2,1,0:T(8,128)(2,1)} copy(bf16[1,16,16,1024]{3,2,1,0:T(8,128)(2,1)} %bitcast.2) | data formatting | bytes 1048576

commit v3 on v2

--- a/solution.py
+++ b/solution.py
@@ -26,10 +26,10 @@
 
 
 def kernel(
-    x_ref, wq_ref, wk_ref, wv_ref, wo_ref, codes_ref, counts_ref, out_ref,
-    xs, wq, wk, wv, wo, wvt, qz, ks, vt, os_, ms, bias, snd, full,
+    x_ref, wq_ref, wk_ref, wv_ref, wo_ref, codes_hbm, counts_hbm, out_ref,
+    codes_ref, counts_ref, xs, wq, wk, wv, wo, wvt, qz, ks, vt, os_, ms, bias, snd, full,
     s0, s1, s2, s3, s4, s5, s6, s7,
-    w_sem, x_sem,
+    w_sem, x_sem, c_sem,
     p_ss, p_rs, y_ss, y_rs, n0_ss, n0_rs, n1_ss, n1_rs, f_ss, f_rs, b_ss, b_rs, a_ss, a_rs,
 ):
     f32, bf16 = jnp.float32, jnp.bfloat16
@@ -48,10 +48,10 @@
         pltpu.make_async_copy(wq_ref.at[:, cols], wq, w_sem.at[2]),
         pltpu.make_async_copy(wo_ref, wo, w_sem.at[3]),
     ]
-    for copy in x_copies:
-        copy.start()
-    for copy in w_copies:
-        copy.start()
+    c_copies = [
+        pltpu.make_async_copy(codes_hbm, codes_ref, c_sem.at[0]),
+        pltpu.make_async_copy(counts_hbm, counts_ref, c_sem.at[1]),
+    ]
 
     def remote(src, dst, ss, rs, dev):
         return pltpu.make_async_remote_copy(
@@ -109,29 +109,8 @@
         pl.when(has_prev)(lambda: greet({"frame": frame - 1}))
         pl.when(has_next)(lambda: greet({"frame": frame + 1}))
 
-    ri = lax.broadcasted_iota(jnp.int32, (8, TOK), 0)
-    li = lax.broadcasted_iota(jnp.int32, (8, TOK), 1)
-    second = (li // TILE) % 2 == 1
-    gcol = 2 * c + (li // TILE) % 2
-    wcol = (ri - gcol + 5) % 4
-    first_ext = []
-    outer = [jnp.where(has_n, 0, 3), jnp.where(has_s, 3, 0)]
-    for r in range(2):
-        first = jnp.minimum(jnp.maximum(2 * lat + r - 1, 0), 2 * nlat - 3) - 2 * lat + 1
-        first_ext.append(first)
-        cnt = jnp.where(second, counts_ref[0, r, 1], counts_ref[0, r, 0])
-        for slot in range(3):
-            ext = outer[r] if slot == 0 else slot
-            want = jnp.where(jnp.logical_and(wcol < 3, ri < 4), 3 * (ext - first) + wcol, -1)
-            live = jnp.zeros((8, TOK), f32)
-            for j in range(WIN):
-                code = jnp.where(second, codes_ref[0, r, 1, j], codes_ref[0, r, 0, j])
-                hit = jnp.logical_and(code == want, j < cnt)
-                live = jnp.where(hit, 1.0, live)
-            bias[c, r, slot] = jnp.where(live > 0.5, 0.0, DEAD)
-    vt[:, :, :, HEAD:, :] = jnp.ones((2, 4, 8, VROWS - HEAD, 2 * TOK), bf16)
-    w_copies[0].wait()
-    wvt[...] = wv[...].T
+    for copy in x_copies + c_copies + w_copies:
+        copy.start()
 
     if COMM:
         greeted = (
@@ -162,52 +141,95 @@
             for i in range(NC):
                 to_next(1, i).start()
 
+
+    ri = lax.broadcasted_iota(jnp.int32, (8, TOK), 0)
+    li = lax.broadcasted_iota(jnp.int32, (8, TOK), 1)
+    second = (li // TILE) % 2 == 1
+    gcol = 2 * c + (li // TILE) % 2
+    wcol = (ri - gcol + 5) % 4
+    for copy in c_copies:
+        copy.wait()
+    outer = [jnp.where(has_n, 0, 3), jnp.where(has_s, 3, 0)]
+    for r in range(2):
+        first = jnp.minimum(jnp.maximum(2 * lat + r - 1, 0), 2 * nlat - 3) - 2 * lat + 1
+        cnt = jnp.where(second, counts_ref[0, r, 1], counts_ref[0, r, 0])
+        for slot in range(3):
+            ext = outer[r] if slot == 0 else slot
+            want = jnp.where(jnp.logical_and(wcol < 3, ri < 4), 3 * (ext - first) + wcol, -1)
+            live = jnp.zeros((8, TOK), f32)
+            for j in range(WIN):
+                code = jnp.where(second, codes_ref[0, r, 1, j], codes_ref[0, r, 0, j])
+                hit = jnp.logical_and(code == want, j < cnt)
+                live = jnp.where(hit, 1.0, live)
+            bias[c, r, slot] = jnp.where(live > 0.5, 0.0, DEAD)
+    if COMM:
         bias_to_peer(c).start()
-
-    def pump_own_sides(i):
+    vt[:, :, :, :, HEAD:, :] = jnp.ones((2, 4, 2, 8, VROWS - HEAD, TOK), bf16)
+    w_copies[0].wait()
+    wvt[...] = wv[...].T
+
+    def quarter(i):
+        return [i * (NC // 4) + k for k in range(NC // 4)]
+
+    def pump_own_sides(q):
+        if not COMM:
+            return
         for side in range(2):
 
             @pl.when(gets_from[side])
             def _(side=side):
-                own_to_side(side, i).wait_recv()
-                forward(0, 3 - 3 * side, i, c).start()
-
-    def pump_prev(r, i):
+                for i in quarter(q):
+                    own_to_side(side, i).wait_recv()
+                    forward(0, 3 - 3 * side, i, c).start()
+
+    def pump_prev(r, q):
+        if not COMM:
+            return
+
         @pl.when(has_prev)
         def _():
-            to_next(r, i).wait_recv()
-
-            @pl.when(send_to[r])
-            def _():
-                prev_to_side(r, i).start()
-
-            forward(1, 1 + r, i, c).start()
-
-    def pump_prev_side(side, i):
-        prev_to_side(side, i).wait_recv()
-        forward(1, 3 - 3 * side, i, c).start()
-
-    def project(x, fr, blk):
+            for i in quarter(q):
+                to_next(r, i).wait_recv()
+
+                @pl.when(send_to[r])
+                def _():
+                    prev_to_side(r, i).start()
+
+                forward(1, 1 + r, i, c).start()
+
+    def pump_prev_side(side, q):
+        if COMM:
+            for i in quarter(q):
+                prev_to_side(side, i).wait_recv()
+                forward(1, 3 - 3 * side, i, c).start()
+
+    def await_forward(fr, row):
+        if COMM:
+            for i in range(NC):
+                forward(fr, row, i, o).wait_recv()
+
+    def project(fr, pieces):
+        x = jnp.concatenate([xs[fr, row, lon] for row, lon in pieces], axis=0)
         key = jnp.dot(x, wk[...], preferred_element_type=f32).astype(bf16)
-        for pair in range(4):
-            ks[fr, blk, pair] = key[:, pair * 128 : (pair + 1) * 128]
         value = lax.dot_general(wvt[...], x, NT, preferred_element_type=f32).astype(bf16)
-        vt[fr, blk, :, :HEAD, :] = value.reshape(8, HEAD, 2 * TOK)
-
-    def row_of(fr, row):
-        return xs[fr, row].reshape(2 * TOK, D)
-
-    def attend(fr, blocks, r, first, group, ahead):
+        for u, (row, lon) in enumerate(pieces):
+            for pair in range(4):
+                ks[fr, row, lon, pair] = key[u * TOK : (u + 1) * TOK, pair * 128 : (pair + 1) * 128]
+            vt[fr, row, lon, :, :HEAD, :] = value[:, u * TOK : (u + 1) * TOK].reshape(8, HEAD, TOK)
+        return x
+
+    def attend(blocks, r, first, group, ahead):
         n = len(blocks)
         masks = []
-        for _, (a, b) in blocks:
-            rows = [jnp.concatenate([bias[0, r, slot], bias[1, r, slot]], axis=1)[k : k + 2] for slot, k in (a, b)]
-            masks.append([v.reshape(2, 1, 2 * TOK) for v in rows])
+        for _, _, slot in blocks:
+            rows = jnp.concatenate([bias[0, r, slot], bias[1, r, slot]], axis=1)
+            masks.append([rows[2 * u : 2 * u + 2].reshape(2, 1, 2 * TOK) for u in range(2)])
 
         def scores(h):
             best = None
-            for k, (blk, _) in enumerate(blocks):
-                s = lax.dot_general(ks[fr, blk, h // 2], qz[r, h], NT, preferred_element_type=f32)
+            for k, (fr, row, _) in enumerate(blocks):
+                key = jnp.concatenate([ks[fr, row, 0, h // 2], ks[fr, row, 1, h // 2]], axis=0)
+                s = lax.dot_general(key, qz[r, h], NT, preferred_element_type=f32)
                 ss[(h * n + k) % 8][...] = s
                 s = s.reshape(2, TILE, 2, TILE, 2 * TOK)
                 for u in range(2):
@@ -221,10 +243,11 @@
 
         def values(h, m, m_old):
             total = None
-            for k, (blk, _) in enumerate(blocks):
+            for k, (fr, row, _) in enumerate(blocks):
                 s = ss[(h * n + k) % 8][...].reshape(2, TILE, 2, TILE, 2 * TOK)
                 p = [jnp.exp(s[u] + (masks[k][u] - m)[None]).reshape(TOK, 2 * TOK).astype(bf16) for u in range(2)]
-                t = jnp.dot(vt[fr, blk, h], jnp.concatenate(p, axis=0), preferred_element_type=f32)
+                value = jnp.concatenate([vt[fr, row, 0, h], vt[fr, row, 1, h]], axis=1)
+                t = jnp.dot(value, jnp.concatenate(p, axis=0), preferred_element_type=f32)
                 total = t if total is None else total + t
             if not first:
                 total = total + os_[r, h] * jnp.exp(m_old - m)
@@ -258,8 +281,7 @@
                     own_to_peer(r, o).wait_recv()
                 bias_to_peer(o).wait_recv()
 
-        x = jnp.concatenate([xs[0, 1, lon], xs[0, 2, lon]], axis=0)
-        project(x, 0, 1 + lon)
+        x = project(0, [(1, lon), (2, lon)])
         query = jnp.dot(x, wq[...], preferred_element_type=f32).astype(bf16).astype(f32) * 0.125
         place = pl.ds(pl.multiple_of(lon * TOK, TOK), TOK)
         for r in range(2):
@@ -270,67 +292,70 @@
 
     @pl.loop(0, 2)
     def _(r):
-        if COMM:
-            for i in range(2):
-                pump_own_sides(2 * r + i)
-                pump_prev(0, 2 * r + i)
-        attend(0, [(1, ((1, 0), (2, 0))), (2, ((1, 2), (2, 2)))], r, True, 2, 1)
-
-    @pl.loop(0, 2)
-    def _(side):
-        @pl.when(jnp.where(side == 0, has_s, has_n))
-        def _():
-            row = 3 - 3 * side
-            if COMM:
-                for i in range(NC):
-                    forward(0, row, i, o).wait_recv()
-            project(row_of(0, row), 0, row)
+        pump_prev(0, r)
+        pump_own_sides(r)
+        attend([(0, 1, 1), (0, 2, 2)], r, True, 2, 1)
+
+    pump_prev(0, 2)
+    pump_own_sides(2)
+    pump_prev(0, 3)
+    pump_own_sides(3)
+
+    project(0, [(0, c), (3, c)])
+    pump_prev(1, 0)
+
+    @pl.when(has_prev)
+    def _():
+        await_forward(1, 1)
+        project(1, [(1, 0), (1, 1)])
+
+    pump_prev(1, 1)
+    for side in range(2):
+        pl.when(gets_from[side])(functools.partial(await_forward, 0, 3 - 3 * side))
+    project(0, [(0, o), (3, o)])
+
+    def outer_of(r):
+        return jnp.where(r == 0, outer[0], outer[1])
 
     @pl.loop(0, 2)
     def _(r):
-        if COMM:
-            pump_prev(1, 2 * r)
-            pump_prev(1, 2 * r + 1)
-        row = jnp.where(r == 0, outer[0], outer[1])
-        attend(0, [(row, ((0, 0), (0, 2)))], r, False, 4, 1)
+        pump_prev(1, 2 + r)
+
+        @pl.when(has_prev)
+        def _():
+            attend([(0, outer_of(r), 0), (1, 1, 1)], r, False, 2, 1)
+
+        @pl.when(jnp.logical_not(has_prev))
+        def _():
+            attend([(0, outer_of(r), 0)], r, False, 4, 1)
+
+    both_sides = jnp.logical_and(has_n, has_s)
 
     @pl.when(has_prev)
     def _():
-        @pl.loop(0, 2)
-        def _(t):
-            row = 1 + t
-            if COMM:
-                for i in range(NC):
-                    forward(1, row, i, o).wait_recv()
-            project(row_of(1, row), 1, row)
-
-            @pl.loop(0, 2)
-            def _(r):
-                attend(1, [(row, ((row, 0), (row, 2)))], r, False, 4, 1)
+        @pl.when(has_s)
+        def _():
+            for i in range(4):
+                pump_prev_side(0, i)
+
+        await_forward(1, 2)
+        project(1, [(2, 0), (2, 1)])
+
+        @pl.when(has_n)
+        def _():
+            for i in range(3):
+                pump_prev_side(1, i)
+
+        attend([(1, 2, 2)], 0, False, 4, 1)
+        pl.when(jnp.logical_not(has_s))(lambda: pump_prev_side(1, 3))
+        row = jnp.where(has_s, 3, 0)
+        await_forward(1, row)
+        project(1, [(row, 0), (row, 1)])
+        attend([(1, 2, 2), (1, outer[1], 0)], 1, False, 2, 1)
 
     mine_first = c == 0
 
-    @pl.loop(0, 2)
-    def _(t):
-        r = 1 - t
-
-        @pl.when(has_prev)
-        def _():
-            row = jnp.where(jnp.logical_and(t == 0, has_s), 3, 0)
-
-            @pl.when(jnp.logical_or(t == 0, jnp.logical_and(has_n, has_s)))
-            def _():
-                if COMM:
-                    side = jnp.where(row == 3, 0, 1)
-                    for i in range(NC):
-                        pump_prev_side(side, i)
-                    for i in range(NC):
-                        forward(1, row, i, o).wait_recv()
-                project(row_of(1, row), 1, row)
-
-            mask_row = jnp.where(r == 0, outer[0], outer[1])
-            attend(1, [(mask_row, ((0, 0), (0, 2)))], r, False, 4, 1)
-
+    def finish(r):
         for h in range(8):
             total = os_[r, h]
             att = (total[:HEAD] * (1.0 / total[HEAD : HEAD + 1])).astype(bf16)
@@ -340,15 +365,30 @@
         if COMM:
             att_to_peer(r, c).start()
 
-    w_copies[3].wait()
-
-    @pl.loop(0, 2)
-    def _(t):
-        r = 1 - t
+    def put_out(r):
         if COMM:
             att_to_peer(r, o).wait_recv()
         a = full[r].reshape(D, TOK)
         out_ref[r] = lax.dot_general(a, wo[...], TN, preferred_element_type=f32).astype(bf16)
+
+    finish(1)
+
+    @pl.when(has_prev)
+    def _():
+        @pl.when(both_sides)
+        def _():
+            pump_prev_side(1, 3)
+            await_forward(1, 0)
+            project(1, [(0, 0), (0, 1)])
+
+        attend([(1, outer[0], 0)], 0, False, 4, 1)
+
+    finish(0)
+    w_copies[3].wait()
+
+    @pl.loop(0, 2)
+    def _(t):
+        put_out(1 - t)
 
     if COMM:
         for r in range(2):
@@ -396,14 +436,14 @@
     x = frames_in.reshape(2, TOK, D)
     bf16, f32 = jnp.bfloat16, jnp.float32
     dma = pltpu.SemaphoreType.DMA
-    anywhere = pl.BlockSpec(memory_space=pl.ANY)
-    scalars = pl.BlockSpec(memory_space=pltpu.SMEM)
     out = pl.pallas_call(
         kernel,
         out_shape=jax.ShapeDtypeStruct((2, TOK, D), bf16),
-        in_specs=[anywhere] * 5 + [scalars] * 2,
+        in_specs=[pl.BlockSpec(memory_space=pltpu.HBM)] * 7,
         out_specs=pl.BlockSpec(memory_space=pltpu.VMEM),
         scratch_shapes=[
+            pltpu.SMEM((1, 2, 2, WIN), jnp.int32),
+            pltpu.SMEM((1, 2, 2), jnp.int32),
             pltpu.VMEM((2, 4, 2, TOK, D), bf16),
             pltpu.VMEM((D, HALF), bf16),
             pltpu.VMEM((D, HALF), bf16),
@@ -411,8 +451,8 @@
             pltpu.VMEM((D, D), bf16),
             pltpu.VMEM((HALF, D), bf16),
             pltpu.VMEM((2, 8, 2 * TOK, 128), bf16),
-            pltpu.VMEM((2, 4, 4, 2 * TOK, 128), bf16),
-            pltpu.VMEM((2, 4, 8, VROWS, 2 * TOK), bf16),
+            pltpu.VMEM((2, 4, 2, 4, TOK, 128), bf16),
+            pltpu.VMEM((2, 4, 2, 8, VROWS, TOK), bf16),
             pltpu.VMEM((2, 8, VROWS, 2 * TOK), f32),
             pltpu.VMEM((2, 8, 8, 2 * TOK), f32),
             pltpu.VMEM((2, 2, 3, 8, TOK), f32),
@@ -420,6 +460,7 @@
             pltpu.VMEM((2, 2, HALF, TOK), bf16),
             *([pltpu.VMEM((2 * TOK, 2 * TOK), f32)] * 8),
             dma((4,)),
+            dma((2,)),
             dma((2,)),
             dma((2,)),
             dma((2,)),
@@ -437,11 +478,11 @@
             dma((2,)),
         ],
         compiler_params=pltpu.CompilerParams(
-            vmem_limit_bytes=60 << 20,
+            vmem_limit_bytes=44 << 20,
             **(dict(collective_id=0, has_side_effects=True) if COMM else {}),
         ),
         cost_estimate=pl.CostEstimate(flops=12 * 10**9, bytes_accessed=8 << 20, transcendentals=6 << 20),
-    )(x, w_query, w_key, w_value, w_out, codes, counts)
+    )(*[pltpu.with_memory_space_constraint(v, pltpu.HBM) for v in (x, w_query, w_key, w_value, w_out, codes, counts)])
     return out.reshape(shape)
 
 

time: 34.6 us -> 30.1 us (0.87)
  the two profiles are of different devices: /device:TPU:111 before, /device:TPU:144 now
where the time goes in v3:
time: 30.1 us
  Pallas kernels  29.2 us (97%)
  local copies, waits for them, and re-layouts  0.8 us (3%)
    pallas_call x1, Pallas kernels, on_device(): pl.pallas_call(kernel, out_shape=jax.ShapeDtypeStruct((2, TOK, D), bf16),...  29.2 us
    unnamed x1, local copies, waits for them, and re-layouts  0.8 us

profile of v3, /device:TPU:144, one launch (start us, length us, event | category | flops | bytes accessed | tf_op | source)
XLA Modules:
  0.0 30.1 jit_solution(8059761501113749114)
XLA Ops:
  0.0 29.2 %shard_map.73 = bf16[2,128,1024]{2,1,0:T(8,128)(2,1)S(1)} custom-call(bf16[2,128,1024]{2,1,0:T(8,128)(2,1)} %bitcast.3, bf16[1024,1024]{1,0:T(8,128)(2,1)} %wq_ref.1, bf16[1024,1024]{1,0:T(8,128)(2,1)} %wk_ref.1, bf16[1024,1024]{1,0:T(8,128)(2,1)} %wv_ref.1, bf16[1024,1024]{1,0:T(8,128)(2,1)} %wo_ref.1, s32[1,2,2,9]{3,2,1,0:T(2,128)} %codes_hbm.1, ...), custom_call_target="tpu_custom_call" | custom-call | flops 12000000000 | bytes 8388608 | tf_op jit(solution)/shard_map/pallas_call | solution.py:439
  29.3 0.8 %copy.9 = bf16[1,16,16,1024]{3,2,1,0:T(8,128)(2,1)} copy(bf16[1,16,16,1024]{3,2,1,0:T(8,128)(2,1)S(1)} %bitcast.2) | data formatting | bytes 1048576

commit v4 on v3

--- a/solution.py
+++ b/solution.py
@@ -15,7 +15,7 @@
 HALF = D // 2
 TOK = 128
 NC = 4
-CH = TOK // NC
+BIG, SMALL = 32, 32
 VROWS = HEAD + 16
 DEAD = -1e38
 FLOOR = -1e30
@@ -58,34 +58,38 @@
             src_ref=src, dst_ref=dst, send_sem=ss, recv_sem=rs, device_id=dev, device_id_type=MESH
         )
 
-    def part(i):
-        return pl.ds(pl.multiple_of(i * CH, CH), CH)
+    def part(i, size):
+        start = BIG * i if size == BIG else 2 * BIG + SMALL * (i - 2)
+        return pl.ds(pl.multiple_of(start, 16), size)
+
+    def pieces():
+        return [(i, BIG if i < 2 else SMALL) for i in range(NC)]
 
     def own_to_peer(r, lon):
         return remote(x_ref.at[r], xs.at[0, 1 + r, lon], p_ss.at[r], p_rs.at[r], {"lon": o})
 
-    def to_next(r, i):
+    def to_next(r, i, size):
         k = r * NC + i
-        return remote(x_ref.at[r, part(i)], xs.at[1, 1 + r, c, part(i)], y_ss.at[k], y_rs.at[k], {"frame": frame + 1})
+        return remote(x_ref.at[r, part(i, size)], xs.at[1, 1 + r, c, part(i, size)], y_ss.at[k], y_rs.at[k], {"frame": frame + 1})
 
     def side_dev(side):
         return {"lat": lat - 1 + 2 * side}
 
-    def own_to_side(side, i):
+    def own_to_side(side, i, size):
         k = side * NC + i
         return remote(
-            x_ref.at[side, part(i)], xs.at[0, 3 - 3 * side, c, part(i)], n0_ss.at[k], n0_rs.at[k], side_dev(side)
+            x_ref.at[side, part(i, size)], xs.at[0, 3 - 3 * side, c, part(i, size)], n0_ss.at[k], n0_rs.at[k], side_dev(side)
         )
 
-    def prev_to_side(side, i):
+    def prev_to_side(side, i, size):
         k = side * NC + i
         return remote(
-            xs.at[1, 1 + side, c, part(i)], xs.at[1, 3 - 3 * side, c, part(i)], n1_ss.at[k], n1_rs.at[k], side_dev(side)
+            xs.at[1, 1 + side, c, part(i, size)], xs.at[1, 3 - 3 * side, c, part(i, size)], n1_ss.at[k], n1_rs.at[k], side_dev(side)
         )
 
-    def forward(fr, row, i, lon):
+    def forward(fr, row, i, size, lon):
         k = (fr * 4 + row) * NC + i
-        block = xs.at[fr, row, lon, part(i)]
+        block = xs.at[fr, row, lon, part(i, size)]
         return remote(block, block, f_ss.at[k], f_rs.at[k], {"lon": o})
 
     def bias_to_peer(lon):
@@ -96,6 +100,8 @@
 
     send_to = (has_n, has_s)
     gets_from = (has_s, has_n)
+    ra = jnp.where(lat % 4 == 3, 1, 0)
+    rb = 1 - ra
 
     if COMM:
         barrier = pltpu.get_barrier_semaphore()
@@ -126,21 +132,20 @@
 
         @pl.when(has_next)
         def _():
-            for i in range(NC):
-                to_next(0, i).start()
+            for i, size in pieces():
+                to_next(ra, i, size).start()
 
         for side in range(2):
 
             @pl.when(send_to[side])
             def _(side=side):
-                for i in range(NC):
-                    own_to_side(side, i).start()
+                for i, size in pieces():
+                    own_to_side(side, i, size).start()
 
         @pl.when(has_next)
         def _():
-            for i in range(NC):
-                to_next(1, i).start()
-
+            for i, size in pieces():
+                to_next(rb, i, size).start()
 
     ri = lax.broadcasted_iota(jnp.int32, (8, TOK), 0)
     li = lax.broadcasted_iota(jnp.int32, (8, TOK), 1)
@@ -168,45 +173,43 @@
     w_copies[0].wait()
     wvt[...] = wv[...].T
 
-    def quarter(i):
-        return [i * (NC // 4) + k for k in range(NC // 4)]
-
-    def pump_own_sides(q):
+    def pump_own_sides(i, size):
         if not COMM:
             return
         for side in range(2):
 
             @pl.when(gets_from[side])
             def _(side=side):
-                for i in quarter(q):
-                    own_to_side(side, i).wait_recv()
-                    forward(0, 3 - 3 * side, i, c).start()
-
-    def pump_prev(r, q):
+                own_to_side(side, i, size).wait_recv()
+                forward(0, 3 - 3 * side, i, size, c).start()
+
+    def pump_prev(r, i, size):
         if not COMM:
             return
 
         @pl.when(has_prev)
         def _():
-            for i in quarter(q):
-                to_next(r, i).wait_recv()
-
-                @pl.when(send_to[r])
-                def _():
-                    prev_to_side(r, i).start()
-
-                forward(1, 1 + r, i, c).start()
-
-    def pump_prev_side(side, q):
-        if COMM:
-            for i in quarter(q):
-                prev_to_side(side, i).wait_recv()
-                forward(1, 3 - 3 * side, i, c).start()
+            to_next(r, i, size).wait_recv()
+
+            @pl.when(jnp.where(r == 0, has_n, has_s))
+            def _():
+                prev_to_side(r, i, size).start()
+
+            forward(1, 1 + r, i, size, c).start()
+
+    def pump_prev_side(side, i, size):
+        if not COMM:
+            return
+
+        @pl.when(gets_from[side])
+        def _():
+            prev_to_side(side, i, size).wait_recv()
+            forward(1, 3 - 3 * side, i, size, c).start()
 
     def await_forward(fr, row):
         if COMM:
-            for i in range(NC):
-                forward(fr, row, i, o).wait_recv()
+            for i, size in pieces():
+                forward(fr, row, i, size, o).wait_recv()
 
     def project(fr, pieces):
         x = jnp.concatenate([xs[fr, row, lon] for row, lon in pieces], axis=0)
@@ -292,24 +295,23 @@
 
     @pl.loop(0, 2)
     def _(r):
-        pump_prev(0, r)
-        pump_own_sides(r)
+        pump_prev(ra, r, BIG)
+        pump_own_sides(r, BIG)
         attend([(0, 1, 1), (0, 2, 2)], r, True, 2, 1)
 
-    pump_prev(0, 2)
-    pump_own_sides(2)
-    pump_prev(0, 3)
-    pump_own_sides(3)
+    for i in range(2, 4):
+        pump_prev(ra, i, SMALL)
+        pump_own_sides(i, SMALL)
 
     project(0, [(0, c), (3, c)])
-    pump_prev(1, 0)
+    pump_prev(rb, 0, BIG)
 
     @pl.when(has_prev)
     def _():
-        await_forward(1, 1)
-        project(1, [(1, 0), (1, 1)])
-
-    pump_prev(1, 1)
+        await_forward(1, 1 + ra)
+        project(1, [(1 + ra, 0), (1 + ra, 1)])
+        pump_prev(rb, 1, BIG)
+
     for side in range(2):
         pl.when(gets_from[side])(functools.partial(await_forward, 0, 3 - 3 * side))
     project(0, [(0, o), (3, o)])
@@ -319,11 +321,11 @@
 
     @pl.loop(0, 2)
     def _(r):
-        pump_prev(1, 2 + r)
+        pump_prev(rb, 2 + r, SMALL)
 
         @pl.when(has_prev)
         def _():
-            attend([(0, outer_of(r), 0), (1, 1, 1)], r, False, 2, 1)
+            attend([(0, outer_of(r), 0), (1, 1 + ra, 1 + ra)], r, False, 2, 1)
 
         @pl.when(jnp.logical_not(has_prev))
         def _():
@@ -333,25 +335,24 @@
 
     @pl.when(has_prev)
     def _():
-        @pl.when(has_s)
-        def _():
-            for i in range(4):
-                pump_prev_side(0, i)
-
-        await_forward(1, 2)
-        project(1, [(2, 0), (2, 1)])
-
-        @pl.when(has_n)
-        def _():
-            for i in range(3):
-                pump_prev_side(1, i)
-
-        attend([(1, 2, 2)], 0, False, 4, 1)
-        pl.when(jnp.logical_not(has_s))(lambda: pump_prev_side(1, 3))
-        row = jnp.where(has_s, 3, 0)
-        await_forward(1, row)
-        project(1, [(row, 0), (row, 1)])
-        attend([(1, 2, 2), (1, outer[1], 0)], 1, False, 2, 1)
+        await_forward(1, 1 + rb)
+        project(1, [(1 + rb, 0), (1 + rb, 1)])
+        for side in range(2):
+            for i in range(2):
+                pump_prev_side(side, i, BIG)
+        @pl.loop(0, 2)
+        def _(r):
+            attend([(1, 1 + rb, 1 + rb)], r, False, 4, 1)
+
+        for i in range(2, 4):
+            for side in range(2):
+                pump_prev_side(side, i, SMALL)
+
+        project(1, [(0, c), (3, c)])
+        for side in range(2):
+            pl.when(gets_from[side])(functools.partial(await_forward, 1, 3 - 3 * side))
+        project(1, [(0, o), (3, o)])
+        attend([(1, outer[1], 0)], 1, False, 4, 1)
 
     mine_first = c == 0
 
@@ -375,12 +376,6 @@
 
     @pl.when(has_prev)
     def _():
-        @pl.when(both_sides)
-        def _():
-            pump_prev_side(1, 3)
-            await_forward(1, 0)
-            project(1, [(0, 0), (0, 1)])
-
         attend([(1, outer[0], 0)], 0, False, 4, 1)
 
     finish(0)
@@ -399,36 +394,36 @@
         @pl.when(has_next)
         def _():
             for r in range(2):
-                for i in range(NC):
-                    to_next(r, i).wait_send()
+                for i, size in pieces():
+                    to_next(r, i, size).wait_send()
 
         for side in range(2):
 
             @pl.when(send_to[side])
             def _(side=side):
-                for i in range(NC):
-                    own_to_side(side, i).wait_send()
+                for i, size in pieces():
+                    own_to_side(side, i, size).wait_send()
 
             @pl.when(gets_from[side])
             def _(side=side):
-                for i in range(NC):
-                    forward(0, 3 - 3 * side, i, c).wait_send()
+                for i, size in pieces():
+                    forward(0, 3 - 3 * side, i, size, c).wait_send()
 
         @pl.when(has_prev)
         def _():
             for side in range(2):
-                for i in range(NC):
-                    forward(1, 1 + side, i, c).wait_send()
+                for i, size in pieces():
+                    forward(1, 1 + side, i, size, c).wait_send()
 
                 @pl.when(send_to[side])
                 def _(side=side):
-                    for i in range(NC):
-                        prev_to_side(side, i).wait_send()
+                    for i, size in pieces():
+                        prev_to_side(side, i, size).wait_send()
 
                 @pl.when(gets_from[side])
                 def _(side=side):
-                    for i in range(NC):
-                        forward(1, 3 - 3 * side, i, c).wait_send()
+                    for i, size in pieces():
+                        forward(1, 3 - 3 * side, i, size, c).wait_send()
 
 
 def on_device(frames_in, w_query, w_key, w_value, w_out, codes, counts):

time: 30.1 us -> 28 us (0.930)
  the two profiles are of different devices: /device:TPU:144 before, /device:TPU:117 now
where the time goes in v4:
time: 28 us; the launch traced here: 27.9 us
  Pallas kernels  27.1 us (97%)
  local copies, waits for them, and re-layouts  0.8 us (3%)
    pallas_call x1, Pallas kernels, on_device(): pl.pallas_call(kernel, out_shape=jax.ShapeDtypeStruct((2, TOK, D), bf16),...  27.1 us
    unnamed x1, local copies, waits for them, and re-layouts  0.8 us

profile of v4, /device:TPU:117, one launch (start us, length us, event | category | flops | bytes accessed | tf_op | source)
XLA Modules:
  0.0 27.9 jit_solution(17680947239800228210)
XLA Ops:
  0.0 27.1 %shard_map.73 = bf16[2,128,1024]{2,1,0:T(8,128)(2,1)S(1)} custom-call(bf16[2,128,1024]{2,1,0:T(8,128)(2,1)} %bitcast.3, bf16[1024,1024]{1,0:T(8,128)(2,1)} %wq_ref.1, bf16[1024,1024]{1,0:T(8,128)(2,1)} %wk_ref.1, bf16[1024,1024]{1,0:T(8,128)(2,1)} %wv_ref.1, bf16[1024,1024]{1,0:T(8,128)(2,1)} %wo_ref.1, s32[1,2,2,9]{3,2,1,0:T(2,128)} %codes_hbm.1, ...), custom_call_target="tpu_custom_call" | custom-call | flops 12000000000 | bytes 8388608 | tf_op jit(solution)/shard_map/pallas_call | solution.py:434
  27.1 0.8 %copy.9 = bf16[1,16,16,1024]{3,2,1,0:T(8,128)(2,1)} copy(bf16[1,16,16,1024]{3,2,1,0:T(8,128)(2,1)S(1)} %bitcast.2) | data formatting | bytes 1048576

commit v5 on v4

--- a/solution.py
+++ b/solution.py
@@ -27,7 +27,7 @@
 
 def kernel(
     x_ref, wq_ref, wk_ref, wv_ref, wo_ref, codes_hbm, counts_hbm, out_ref,
-    codes_ref, counts_ref, xs, wq, wk, wv, wo, wvt, qz, ks, vt, os_, ms, bias, snd, full,
+    codes_ref, counts_ref, xs, wq, wk, wv, wo, wvt, qz, ks, vt, os_, ms, bias, snd, full, part_out,
     s0, s1, s2, s3, s4, s5, s6, s7,
     w_sem, x_sem, c_sem,
     p_ss, p_rs, y_ss, y_rs, n0_ss, n0_rs, n1_ss, n1_rs, f_ss, f_rs, b_ss, b_rs, a_ss, a_rs,
@@ -366,11 +366,14 @@
         if COMM:
             att_to_peer(r, c).start()
 
+    def half_out(r, half):
+        rows = pl.ds(pl.multiple_of(half * HALF, HALF), HALF)
+        return lax.dot_general(full[r, half], wo[rows, :], TN, preferred_element_type=f32)
+
     def put_out(r):
         if COMM:
             att_to_peer(r, o).wait_recv()
-        a = full[r].reshape(D, TOK)
-        out_ref[r] = lax.dot_general(a, wo[...], TN, preferred_element_type=f32).astype(bf16)
+        out_ref[r] = (part_out[r] + half_out(r, o)).astype(bf16)
 
     finish(1)
 
@@ -380,6 +383,10 @@
 
     finish(0)
     w_copies[3].wait()
+
+    @pl.loop(0, 2)
+    def _(r):
+        part_out[r] = half_out(r, c)
 
     @pl.loop(0, 2)
     def _(t):
@@ -453,6 +460,7 @@
             pltpu.VMEM((2, 2, 3, 8, TOK), f32),
             pltpu.VMEM((2, HALF, TOK), bf16),
             pltpu.VMEM((2, 2, HALF, TOK), bf16),
+            pltpu.VMEM((2, TOK, D), f32),
             *([pltpu.VMEM((2 * TOK, 2 * TOK), f32)] * 8),
             dma((4,)),
             dma((2,)),

time: 28 us -> 27.9 us (level)
  the two profiles are of different devices: /device:TPU:117 before, /device:TPU:111 now
where the time goes in v5:
time: 27.9 us; the launch traced here: 27.4 us
  Pallas kernels  26.6 us (95%)
  local copies, waits for them, and re-layouts  0.8 us (3%)
    pallas_call x1, Pallas kernels, on_device(): pl.pallas_call(kernel, out_shape=jax.ShapeDtypeStruct((2, TOK, D), bf16),...  26.6 us
    unnamed x1, local copies, waits for them, and re-layouts  0.8 us

profile of v5, /device:TPU:111, one launch (start us, length us, event | category | flops | bytes accessed | tf_op | source)
XLA Modules:
  0.0 27.4 jit_solution(6411913170733050857)
XLA Ops:
  0.0 26.6 %shard_map.73 = bf16[2,128,1024]{2,1,0:T(8,128)(2,1)S(1)} custom-call(bf16[2,128,1024]{2,1,0:T(8,128)(2,1)} %bitcast.3, bf16[1024,1024]{1,0:T(8,128)(2,1)} %wq_ref.1, bf16[1024,1024]{1,0:T(8,128)(2,1)} %wk_ref.1, bf16[1024,1024]{1,0:T(8,128)(2,1)} %wv_ref.1, bf16[1024,1024]{1,0:T(8,128)(2,1)} %wo_ref.1, s32[1,2,2,9]{3,2,1,0:T(2,128)} %codes_hbm.1, ...), custom_call_target="tpu_custom_call" | custom-call | flops 12000000000 | bytes 8388608 | tf_op jit(solution)/shard_map/pallas_call | solution.py:441
  26.7 0.8 %copy.9 = bf16[1,16,16,1024]{3,2,1,0:T(8,128)(2,1)} copy(bf16[1,16,16,1024]{3,2,1,0:T(8,128)(2,1)S(1)} %bitcast.2) | data formatting | bytes 1048576

commit v6 on v5

--- a/solution.py
+++ b/solution.py
@@ -295,8 +295,8 @@
 
     @pl.loop(0, 2)
     def _(r):
+        pump_own_sides(r, BIG)
         pump_prev(ra, r, BIG)
-        pump_own_sides(r, BIG)
         attend([(0, 1, 1), (0, 2, 2)], r, True, 2, 1)
 
     for i in range(2, 4):

time: 27.9 us -> 27.9 us (level)
  no operation moved by 1% of the time
where the time goes in v6:
time: 27.9 us; the launch traced here: 27.4 us
  Pallas kernels  26.6 us (95%)
  local copies, waits for them, and re-layouts  0.8 us (3%)
    pallas_call x1, Pallas kernels, on_device(): pl.pallas_call(kernel, out_shape=jax.ShapeDtypeStruct((2, TOK, D), bf16),...  26.6 us
    unnamed x1, local copies, waits for them, and re-layouts  0.8 us

profile of v6, /device:TPU:111, one launch (start us, length us, event | category | flops | bytes accessed | tf_op | source)
XLA Modules:
  0.0 27.4 jit_solution(2821190634965932510)
XLA Ops:
  0.0 26.6 %shard_map.73 = bf16[2,128,1024]{2,1,0:T(8,128)(2,1)S(1)} custom-call(bf16[2,128,1024]{2,1,0:T(8,128)(2,1)} %bitcast.3, bf16[1024,1024]{1,0:T(8,128)(2,1)} %wq_ref.1, bf16[1024,1024]{1,0:T(8,128)(2,1)} %wk_ref.1, bf16[1024,1024]{1,0:T(8,128)(2,1)} %wv_ref.1, bf16[1024,1024]{1,0:T(8,128)(2,1)} %wo_ref.1, s32[1,2,2,9]{3,2,1,0:T(2,128)} %codes_hbm.1, ...), custom_call_target="tpu_custom_call" | custom-call | flops 12000000000 | bytes 8388608 | tf_op jit(solution)/shard_map/pallas_call | solution.py:441
  26.7 0.8 %copy.9 = bf16[1,16,16,1024]{3,2,1,0:T(8,128)(2,1)} copy(bf16[1,16,16,1024]{3,2,1,0:T(8,128)(2,1)S(1)} %bitcast.2) | data formatting | bytes 1048576
